TPU v7x, 512 devices: a whole 4x8x8 slice. The times are simulated.
512 devices in a mesh: row: 16 (over z, core), col: 32 (over y, x).
Axes of the slice: x: 4, y: 8, z: 8, core: 2. Of those that a mesh axis runs over, the one named last changes fastest.
Arguments:
- primal: float32 [8, 131072], P(None, ('col', 'row')), may hold values from 0 to 0.5
- dual: float32 [8, 131072], P(None, ('row', 'col')), may hold values from 0 to 1
- cost: float32 [8, 131072], P(None, ('col', 'row')), may hold values from -6 to 6
- upper: float32 [131072], P(('col', 'row')), may hold values from 0.25 to 1.5
- rhs: float32 [131072], P(('row', 'col')), may hold values from -6 to 6
- row_kind: int32 [131072], P(('row', 'col')), may hold values 0 or 1
- tiles: bfloat16 [24576, 128, 128], P(('row', 'col')), may hold values from -0.125 to 0.125
- tile_rows: int32 [24576], P(('row', 'col')), may hold values from 0 to 63, as said below
- tile_cols: int32 [24576], P(('row', 'col')), may hold values from 0 to 31
- tile_count: int32 [512], P(('row', 'col')), may hold values from 1 to 48, as said below
Outputs:
- primal_out: float32 [8, 131072], P(None, ('col', 'row'))
- dual_out: float32 [8, 131072], P(None, ('row', 'col'))
Inputs may be any that keep to these rules, and one draw needn't show every extreme that they name: Within one device's slots the pairs (tile_rows, tile_cols) are all different. `tile_count`: some device has all 48 slots live in every draw; which one varies.
All inputs are finite; a program needn't handle non-finite values. No bound on the sum of `row_kind` on one device may be relied on, other than what follows from the above.
Results may differ from a plain program's by a relative error of at most 0.0012.
Values may be sent and summed in bfloat16 or wider, within the bound.
No kernel may reach another device: no remote copies, remote signals or barrier semaphores. Data moves between devices by JAX's collectives and lax.ppermute only.
A program may use at most 64 MiB of HBM per device.

v0:
```python
import jax
import jax.numpy as jnp
from jax import lax
from jax.sharding import PartitionSpec as P

ITERS = 2


PRIMAL_STEP = 0.4
DUAL_STEP = 0.4


def tile_forward(source, tiles, tile_rows, tile_cols, live, row_tiles):
    width = source.shape[0]
    col_tiles = source.shape[1] // 128
    pieces = source.reshape(width, col_tiles, 128)[:, tile_cols]
    contrib = jnp.einsum("rtk,tjk->rtj", pieces, tiles, preferred_element_type=jnp.float32)
    onehot = (
        (tile_rows[:, None] == jnp.arange(row_tiles, dtype=jnp.int32)[None, :]) & live[:, None]
    ).astype(jnp.float32)
    return jnp.einsum("rtj,ts->rsj", contrib, onehot, precision=lax.Precision.HIGHEST).reshape(
        width, row_tiles * 128
    )


def tile_adjoint(source, tiles, tile_rows, tile_cols, live, col_tiles):
    width = source.shape[0]
    row_tiles = source.shape[1] // 128
    pieces = source.reshape(width, row_tiles, 128)[:, tile_rows]
    contrib = jnp.einsum("rtj,tjk->rtk", pieces, tiles, preferred_element_type=jnp.float32)
    onehot = (
        (tile_cols[:, None] == jnp.arange(col_tiles, dtype=jnp.int32)[None, :]) & live[:, None]
    ).astype(jnp.float32)
    return jnp.einsum("rtk,ts->rsk", contrib, onehot, precision=lax.Precision.HIGHEST).reshape(
        width, col_tiles * 128
    )


def body(primal, dual, cost, upper, rhs, row_kind, tiles, tile_rows, tile_cols, tile_count):
    row_devices = lax.axis_size("row")
    col_devices = lax.axis_size("col")
    primal_width = primal.shape[1]
    dual_width = dual.shape[1]
    col_tiles = primal_width * row_devices // 128
    row_tiles = dual_width * col_devices // 128
    live = jnp.arange(tiles.shape[0], dtype=jnp.int32) < tile_count[0]
    kind_float = row_kind.astype(jnp.float32)
    state_x, cost_here, upper_here = (primal, cost, upper)
    state_y, rhs_here, kind_here = (dual, rhs, kind_float)
    for step in range(ITERS):
        dual_low = state_y.astype(jnp.bfloat16)
        dual_rows = lax.all_gather(dual_low, "col", axis=1, tiled=True)
        partial_grad = tile_adjoint(dual_rows, tiles, tile_rows, tile_cols, live, col_tiles)
        grad_part = lax.psum_scatter(partial_grad, "row", scatter_dimension=1, tiled=True)
        x_new = jnp.clip(state_x - PRIMAL_STEP * (cost_here - grad_part), 0.0, upper_here[None, :])
        xbar = (2.0 * x_new - state_x).astype(jnp.bfloat16)
        xbar_block = lax.all_gather(xbar, "row", axis=1, tiled=True)
        partial_image = tile_forward(xbar_block, tiles, tile_rows, tile_cols, live, row_tiles)
        image = lax.psum_scatter(partial_image, "col", scatter_dimension=1, tiled=True)
        y_new = state_y + DUAL_STEP * (rhs_here[None, :] - image)
        y_new = jnp.where(kind_here[None, :] > 0.5, jnp.maximum(y_new, 0.0), y_new)
        state_x = x_new
        state_y = y_new
    return (state_x, state_y)


def solution(mesh):
    in_specs = (
        P(None, ("col", "row")),
        P(None, ("row", "col")),
        P(None, ("col", "row")),
        P(("col", "row")),
        P(("row", "col")),
        P(("row", "col")),
        P(("row", "col"), None, None),
        P(("row", "col")),
        P(("row", "col")),
        P(("row", "col")),
    )
    out_specs = (P(None, ("col", "row")), P(None, ("row", "col")))
    return jax.shard_map(body, mesh=mesh, in_specs=in_specs, out_specs=out_specs, check_vma=False)
```

profile of v0, /device:TPU:1, one launch (start us, length us, event | category | flops | bytes accessed | tf_op | source)
XLA Modules:
  0.0 683.3 jit_solution(7515840959926288641)
XLA Ops:
  7.3 0.8 convert_element_type.19
  8.1 32.3 %all_gather.12 = bf16[8,8192]{1,0:T(8,128)(2,1)S(1)} all-gather(bf16[8,256]{1,0:T(8,128)(2,1)S(1)} %convert_element_type.19), channel_id=1, replica_groups=mesh['row'=16,'col'=32] {'col'}, dimensions={1}, use_global_device_ids=true | all-gather | bytes 135168 | tf_op jit(solution)/shard_map/all_gather | solution.py:52
  40.3 0.7 compare_select_fusion.1
  41.7 0.6 gather_fusion
  43.1 0.7 copy.43
  43.9 66.3 %reduce-scatter.5.cloned.1.call-done = f32[8,256]{1,0:T(8,128)} async-done(((f32[8,4096]{1,0:T(8,128)}), f32[8,256]{1,0:T(8,128)}) %reduce-scatter.5.cloned.1.call-update) | async-done | bytes 8208 | tf_op jit(solution)/shard_map/reduce_scatter | solution.py:54
  110.2 0.7 subtract_convert_fusion.1
  110.9 17.6 %all_gather.13 = bf16[8,4096]{1,0:T(8,128)(2,1)S(1)} all-gather(bf16[8,256]{1,0:T(8,128)(2,1)S(1)} %get-tuple-element.4), channel_id=1, replica_groups=mesh['row'=16,'col'=32] {'row'}, dimensions={1}, use_global_device_ids=true | all-gather | bytes 69632 | tf_op jit(solution)/shard_map/all_gather | solution.py:57
  128.5 0.6 gather_fusion.1
  129.2 0.9 fusion.12
  130.5 0.9 copy.41
  131.4 210.9 %reduce-scatter.7.cloned.1.call-done = f32[8,256]{1,0:T(8,128)} async-done(((f32[8,8192]{1,0:T(8,128)}), f32[8,256]{1,0:T(8,128)}) %reduce-scatter.7.cloned.1.call-update) | async-done | bytes 8208 | tf_op jit(solution)/shard_map/reduce_scatter | solution.py:59
  342.3 0.7 fusion.32
  343.0 28.4 %all_gather.14 = bf16[8,8192]{1,0:T(8,128)(2,1)S(1)} all-gather(bf16[8,256]{1,0:T(8,128)(2,1)S(1)} %fusion.32), channel_id=1, replica_groups=mesh['row'=16,'col'=32] {'col'}, dimensions={1}, use_global_device_ids=true | all-gather | bytes 135168 | tf_op jit(solution)/shard_map/all_gather | solution.py:52
  371.4 0.6 gather_fusion.2
  372.8 0.7 copy.42
  373.6 69.3 %reduce-scatter.9.cloned.1.call-done = f32[8,256]{1,0:T(8,128)} async-done(((f32[8,4096]{1,0:T(8,128)}), f32[8,256]{1,0:T(8,128)}) %reduce-scatter.9.cloned.1.call-update) | async-done | bytes 8208 | tf_op jit(solution)/shard_map/reduce_scatter | solution.py:54
  442.9 1.3 subtract_convert_fusion
  444.2 17.6 %all_gather.15 = bf16[8,4096]{1,0:T(8,128)(2,1)S(1)} all-gather(bf16[8,256]{1,0:T(8,128)(2,1)S(1)} %get-tuple-element.2), channel_id=1, replica_groups=mesh['row'=16,'col'=32] {'row'}, dimensions={1}, use_global_device_ids=true | all-gather | bytes 69632 | tf_op jit(solution)/shard_map/all_gather | solution.py:57
  461.8 0.6 gather_fusion.3
  462.5 0.9 fusion.8
  463.8 0.9 copy.40
  464.6 210.8 %reduce-scatter.11.cloned.1.call-done = f32[8,256]{1,0:T(8,128)} async-done(((f32[8,8192]{1,0:T(8,128)}), f32[8,256]{1,0:T(8,128)}) %reduce-scatter.11.cloned.1.call-update) | async-done | bytes 8208 | tf_op jit(solution)/shard_map/reduce_scatter | solution.py:59
  675.4 1.3 maximum_select_fusion
  (39 shorter events, 2.6 us)
Async XLA Ops:
  7.2 35.1 %copy-start = (bf16[48,128,128]{2,1,0:T(8,128)(2,1)S(1)}, bf16[48,128,128]{2,1,0:T(8,128)(2,1)}, u32[]{:S(2)}) copy-start(bf16[48,128,128]{2,1,0:T(8,128)(2,1)} %param.16) | copy-start | bytes 4718596
  7.2 35.6 %copy-start.7 = (s32[48]{0:T(128)S(1)}, s32[48]{0:T(128)}, u32[]{:S(2)}) copy-start(s32[48]{0:T(128)} %param.18) | copy-start | bytes 580
  7.2 103.0 %copy-start.4 = (f32[8,256]{1,0:T(8,128)S(1)}, f32[8,256]{1,0:T(8,128)}, u32[]{:S(2)}) copy-start(f32[8,256]{1,0:T(8,128)} %param.10) | copy-start | bytes 24580
  7.2 103.0 %copy-start.2 = (f32[8,256]{1,0:T(8,128)S(1)}, f32[8,256]{1,0:T(8,128)}, u32[]{:S(2)}) copy-start(f32[8,256]{1,0:T(8,128)} %param.12) | copy-start | bytes 24580
  7.2 103.0 %copy-start.5 = (f32[256]{0:T(256)S(1)}, f32[256]{0:T(256)}, u32[]{:S(2)}) copy-start(f32[256]{0:T(256)} %param.13) | copy-start | bytes 3076
  7.2 102.9 %reduce-scatter.5.cloned.1.call-start = ((), (), s32[]{:S(2)}) async-start(), calls=%async_computation.4 | async-start | bytes 139264 | tf_op jit(solution)/shard_map/reduce_scatter | solution.py:54
  42.8 87.2 %copy-start.8 = (s32[48]{0:T(128)S(1)}, s32[48]{0:T(128)}, u32[]{:S(2)}) copy-start(s32[48]{0:T(128)} %param.17) | copy-start | bytes 580
  43.8 298.5 %reduce-scatter.7.cloned.1.call-start = ((), (), s32[]{:S(2)}) async-start(), calls=%async_computation.5 | async-start | bytes 270336 | tf_op jit(solution)/shard_map/reduce_scatter | solution.py:59
  129.1 2.3 copy-start.9
  129.1 213.2 %copy-start.1 = (f32[8,256]{1,0:T(8,128)S(1)}, f32[8,256]{1,0:T(8,128)}, u32[]{:S(2)}) copy-start(f32[8,256]{1,0:T(8,128)} %param.11) | copy-start | bytes 24580
  129.1 213.2 %copy-start.6 = (f32[256]{0:T(256)S(1)}, f32[256]{0:T(256)}, u32[]{:S(2)}) copy-start(f32[256]{0:T(256)} %param.14) | copy-start | bytes 3076
  131.4 311.6 %reduce-scatter.9.cloned.1.call-start = ((), (), s32[]{:S(2)}) async-start(), calls=%async_computation.6 | async-start | bytes 139264 | tf_op jit(solution)/shard_map/reduce_scatter | solution.py:54
  373.6 301.9 %reduce-scatter.11.cloned.1.call-start = ((), (), s32[]{:S(2)}) async-start(), calls=%async_computation.7 | async-start | bytes 270336 | tf_op jit(solution)/shard_map/reduce_scatter | solution.py:59
  462.4 213.0 %copy-start.3 = (f32[8,256]{1,0:T(8,128)S(1)}, f32[8,256]{1,0:T(8,128)}, u32[]{:S(2)}) copy-start(f32[8,256]{1,0:T(8,128)} %reduce-scatter.7.cloned.1.call-done) | copy-start | bytes 24580
Sparse Core Ops, SparseCore 0:
  43.9 66.1 reduce-scatter.4
  131.5 210.7 reduce-scatter.6
  373.7 69.2 reduce-scatter.8
  464.8 210.5 reduce-scatter.10
where the time goes:
time: 688 us; the launch traced here: 683 us
  waiting for transfers between devices  557 us (81%)
  blocking collectives  95.9 us (14%)
  between operations  14.6 us (2%)
    reduce_scatter x2, waiting for transfers between devices, body(): lax.psum_scatter(partial_image, 'col', scatter_dimension=1, tiled=True)  422 us
    reduce_scatter x2, waiting for transfers between devices, body(): lax.psum_scatter(partial_grad, 'row', scatter_dimension=1, tiled=True)  136 us
    all_gather x2, blocking collectives, body(): dual_rows = lax.all_gather(dual_low, 'col', axis=1, tiled=True)  60.7 us
    all_gather x2, blocking collectives, body(): xbar_block = lax.all_gather(xbar, 'row', axis=1, tiled=True)  35.2 us
  transfers between devices with their start and end apart: 4, of which 4 were waited for; matrix products, arithmetic and copies ran while one was open for 0% of the time, Pallas kernels for 0%

commit v1 on v0

v1 whole, which is shorter than its diff:
```python
import jax
import jax.numpy as jnp
from jax import lax
from jax.sharding import PartitionSpec as P

ITERS = 2
PRIMAL_STEP = 0.4
DUAL_STEP = 0.4
LANES = 128


def to_all(piece, axis):
    copies = jnp.broadcast_to(piece[None], (lax.axis_size(axis), *piece.shape))
    return lax.all_to_all(copies, axis, 0, 0, tiled=True)


def to_owners(parts, axis):
    return jnp.sum(lax.all_to_all(parts, axis, 0, 0, tiled=True).astype(jnp.float32), axis=0)


def as_tiles(slabs):
    devices, width, lanes = slabs.shape
    tiles = slabs.reshape(devices, width, lanes // LANES, LANES).transpose(0, 2, 1, 3)
    return tiles.reshape(-1, width, LANES)


def as_slabs(sums, devices):
    count, width, lanes = sums.shape
    slabs = sums.reshape(devices, count // devices, width, lanes).transpose(0, 2, 1, 3)
    return slabs.reshape(devices, width, -1)


def place(contrib, where, live, count):
    onehot = ((where[:, None] == jnp.arange(count, dtype=jnp.int32)[None, :]) & live[:, None]).astype(jnp.float32)
    return jnp.einsum("trj,ts->srj", contrib, onehot, precision=lax.Precision.HIGHEST)


def body(primal, dual, cost, upper, rhs, row_kind, tiles, tile_rows, tile_cols, tile_count):
    row_devices = lax.axis_size("row")
    col_devices = lax.axis_size("col")
    col_tiles = primal.shape[1] * row_devices // LANES
    row_tiles = dual.shape[1] * col_devices // LANES
    live = jnp.arange(tiles.shape[0], dtype=jnp.int32) < tile_count[0]
    x, y = primal, dual
    for _ in range(ITERS):
        y_rows = as_tiles(to_all(y.astype(jnp.bfloat16), "col"))
        contrib = jnp.einsum("trj,tjk->trk", y_rows[tile_rows], tiles, preferred_element_type=jnp.float32)
        grad = to_owners(as_slabs(place(contrib, tile_cols, live, col_tiles), row_devices), "row")
        x_new = jnp.clip(x - PRIMAL_STEP * (cost - grad), 0.0, upper[None, :])
        xbar = (2.0 * x_new - x).astype(jnp.bfloat16)
        x_cols = as_tiles(to_all(xbar, "row"))
        contrib = jnp.einsum("trk,tjk->trj", x_cols[tile_cols], tiles, preferred_element_type=jnp.float32)
        image = to_owners(as_slabs(place(contrib, tile_rows, live, row_tiles), col_devices), "col")
        y_new = y + DUAL_STEP * (rhs[None, :] - image)
        y = jnp.where(row_kind[None, :] == 1, jnp.maximum(y_new, 0.0), y_new)
        x = x_new
    return x, y


def solution(mesh):
    in_specs = (
        P(None, ("col", "row")),
        P(None, ("row", "col")),
        P(None, ("col", "row")),
        P(("col", "row")),
        P(("row", "col")),
        P(("row", "col")),
        P(("row", "col"), None, None),
        P(("row", "col")),
        P(("row", "col")),
        P(("row", "col")),
    )
    out_specs = (P(None, ("col", "row")), P(None, ("row", "col")))
    return jax.shard_map(body, mesh=mesh, in_specs=in_specs, out_specs=out_specs, check_vma=False)
```

time: 688 us -> 133 us (0.19)
  waiting for transfers between devices: 557 us -> 27.2 us
  blocking collectives: 95.9 us -> 74 us
  starting transfers between devices: 0.16 us -> 17.8 us
  between operations: 14.6 us -> 1.59 us
    reduce_scatter x4 -> x0, waiting for transfers between devices: 557 us -> none  [the longest x2 422 us: body(): lax.psum_scatter(partial_image, 'col', scatter_dimension=1, tiled=True)]
    all_gather x4 -> x0, blocking collectives: 95.9 us -> none  [the longest x2 60.7 us: body(): dual_rows = lax.all_gather(dual_low, 'col', axis=1, tiled=True)]
    all_to_all x0 -> x5, blocking collectives: none -> 74 us  [the longest x3 50.6 us: to_owners(): lax.all_to_all(parts, axis, 0, 0, tiled=True).astype(jnp.float32)]
    all_to_all x0 -> x3, waiting for transfers between devices: none -> 27.2 us  [the longest x2 15.3 us: to_all(): return lax.all_to_all(copies, axis, 0, 0, tiled=True)]
    all_to_all x0 -> x3, starting transfers between devices: none -> 17.8 us  [the longest x2 13.9 us: to_all(): return lax.all_to_all(copies, axis, 0, 0, tiled=True)]
  transfers between devices with their start and end apart: 4 -> 3, of which waited for: 4 -> 3; matrix products, arithmetic and copies ran while one was open for 0% -> 1% of each run, Pallas kernels for 0% -> 0%
where the time goes in v1:
time: 133 us
  blocking collectives  74 us (56%)
  waiting for transfers between devices  27.2 us (20%)
  starting transfers between devices  17.8 us (13%)
  local copies, waits for them, and re-layouts  5 us (4%)
  matrix products  4.08 us (3%)
  other arithmetic  2.93 us (2%)
  between operations  1.59 us (1%)
    all_to_all x3, blocking collectives, to_owners(): lax.all_to_all(parts, axis, 0, 0, tiled=True).astype(jnp.float32)  50.6 us
    all_to_all x2, blocking collectives, to_all(): return lax.all_to_all(copies, axis, 0, 0, tiled=True)  23.4 us
    all_to_all x2, waiting for transfers between devices, to_all(): return lax.all_to_all(copies, axis, 0, 0, tiled=True)  15.3 us
    all_to_all x2, starting transfers between devices, to_all(): return lax.all_to_all(copies, axis, 0, 0, tiled=True)  13.9 us
    all_to_all x1, waiting for transfers between devices, to_owners(): lax.all_to_all(parts, axis, 0, 0, tiled=True).astype(jnp.float32)  12 us
    all_to_all x1, starting transfers between devices, to_owners(): lax.all_to_all(parts, axis, 0, 0, tiled=True).astype(jnp.float32)  3.87 us
  transfers between devices with their start and end apart: 3, of which 3 were waited for; matrix products, arithmetic and copies ran while one was open for 1% of the time, Pallas kernels for 0%

profile of v1, /device:TPU:1, one launch (start us, length us, event | category | flops | bytes accessed | tf_op | source)
XLA Modules:
  0.0 132.6 jit_solution(8009310796687621481)
XLA Ops:
  0.7 0.8 convert_element_type.16
  1.5 0.7 broadcast_in_dim.20
  2.1 10.5 %all-to-all-start = ((bf16[32,8,256]{2,1,0:T(8,128)(2,1)}), bf16[32,8,256]{2,1,0:T(8,128)(2,1)S(1)}, u32[]{:S(2)}, u32[]{:S(2)}) async-start(bf16[32,8,256]{2,1,0:T(8,128)(2,1)} %broadcast_in_dim.20), calls=%async_computation | async-start | bytes 262144 | tf_op jit(solution)/shard_map/all_to_all | solution.py:14
  12.6 0.7 compare_select_fusion.1
  14.0 8.0 %all-to-all-done = bf16[32,8,256]{2,1,0:T(8,128)(2,1)S(1)} async-done(((bf16[32,8,256]{2,1,0:T(8,128)(2,1)}), bf16[32,8,256]{2,1,0:T(8,128)(2,1)S(1)}, u32[]{:S(2)}, u32[]{:S(2)}) %all-to-all-start) | async-done | bytes 131104 | tf_op jit(solution)/shard_map/all_to_all | solution.py:14
  22.1 0.6 gather_fusion
  23.5 21.4 %all_to_all.40 = f32[16,8,256]{2,1,0:T(8,128)S(1)} all-to-all(f32[16,8,256]{2,1,0:T(8,128)S(1)} %bitcast.50), channel_id=1, replica_groups=mesh['row'=16,'col'=32] {'row'}, dimensions={0} | all-to-all | bytes 262144 | tf_op jit(solution)/shard_map/all_to_all | solution.py:18
  45.0 0.6 broadcast_in_dim.26
  45.6 3.4 %all-to-all-start.2 = ((bf16[16,8,256]{2,1,0:T(8,128)(2,1)}), bf16[16,8,256]{2,1,0:T(8,128)(2,1)S(1)}, u32[]{:S(2)}, u32[]{:S(2)}) async-start(bf16[16,8,256]{2,1,0:T(8,128)(2,1)} %broadcast_in_dim.26), calls=%async_computation.2 | async-start | bytes 131072 | tf_op jit(solution)/shard_map/all_to_all | solution.py:14
  49.0 7.2 %all-to-all-done.2 = bf16[16,8,256]{2,1,0:T(8,128)(2,1)S(1)} async-done(((bf16[16,8,256]{2,1,0:T(8,128)(2,1)}), bf16[16,8,256]{2,1,0:T(8,128)(2,1)S(1)}, u32[]{:S(2)}, u32[]{:S(2)}) %all-to-all-start.2) | async-done | bytes 65568 | tf_op jit(solution)/shard_map/all_to_all | solution.py:14
  56.3 0.6 gather_fusion.1
  56.9 0.9 fusion.30
  58.2 0.9 copy.33
  59.1 3.9 %all-to-all-start.3 = ((f32[32,8,256]{2,1,0:T(8,128)}), f32[32,8,256]{2,1,0:T(8,128)S(1)}, u32[]{:S(2)}, u32[]{:S(2)}) async-start(f32[32,8,256]{2,1,0:T(8,128)} %bitcast.42), calls=%async_computation.3 | async-start | bytes 524288 | tf_op jit(solution)/shard_map/all_to_all | solution.py:18
  63.0 12.0 %all-to-all-done.3 = f32[32,8,256]{2,1,0:T(8,128)S(1)} async-done(((f32[32,8,256]{2,1,0:T(8,128)}), f32[32,8,256]{2,1,0:T(8,128)S(1)}, u32[]{:S(2)}, u32[]{:S(2)}) %all-to-all-start.3) | async-done | bytes 262176 | tf_op jit(solution)/shard_map/all_to_all | solution.py:18
  75.1 13.2 %all_to_all.41 = bf16[32,8,256]{2,1,0:T(8,128)(2,1)S(1)} all-to-all(bf16[32,8,256]{2,1,0:T(8,128)(2,1)S(1)} %broadcast_in_dim.28), channel_id=1, replica_groups=mesh['row'=16,'col'=32] {'col'}, dimensions={0} | all-to-all | bytes 262144 | tf_op jit(solution)/shard_map/all_to_all | solution.py:14
  88.3 0.6 gather_fusion.2
  89.8 14.4 %all_to_all.42 = f32[16,8,256]{2,1,0:T(8,128)S(1)} all-to-all(f32[16,8,256]{2,1,0:T(8,128)S(1)} %bitcast.52), channel_id=1, replica_groups=mesh['row'=16,'col'=32] {'row'}, dimensions={0} | all-to-all | bytes 262144 | tf_op jit(solution)/shard_map/all_to_all | solution.py:18
  104.2 0.6 subtract_convert_fusion
  104.9 10.2 %all_to_all.43 = bf16[16,8,256]{2,1,0:T(8,128)(2,1)S(1)} all-to-all(bf16[16,8,256]{2,1,0:T(8,128)(2,1)S(1)} %broadcast_in_dim.29), channel_id=1, replica_groups=mesh['row'=16,'col'=32] {'row'}, dimensions={0} | all-to-all | bytes 131072 | tf_op jit(solution)/shard_map/all_to_all | solution.py:14
  115.1 0.6 gather_fusion.3
  115.7 0.9 fusion.32
  117.2 14.8 %all_to_all.44 = f32[32,8,256]{2,1,0:T(8,128)S(1)} all-to-all(f32[32,8,256]{2,1,0:T(8,128)S(1)} %bitcast.48), channel_id=1, replica_groups=mesh['row'=16,'col'=32] {'col'}, dimensions={0} | all-to-all | bytes 524288 | tf_op jit(solution)/shard_map/all_to_all | solution.py:18
  132.0 0.6 maximum_select_fusion
  (48 shorter events, 2.9 us)
Async XLA Ops:
  0.6 22.0 %copy-start = (bf16[48,128,128]{2,1,0:T(8,128)(2,1)S(1)}, bf16[48,128,128]{2,1,0:T(8,128)(2,1)}, u32[]{:S(2)}) copy-start(bf16[48,128,128]{2,1,0:T(8,128)(2,1)} %param.16) | copy-start | bytes 4718596
  0.6 22.6 %copy-start.6 = (s32[48]{0:T(128)S(1)}, s32[48]{0:T(128)}, u32[]{:S(2)}) copy-start(s32[48]{0:T(128)} %param.18) | copy-start | bytes 580
  2.1 19.9 %all-to-all-start = ((bf16[32,8,256]{2,1,0:T(8,128)(2,1)}), bf16[32,8,256]{2,1,0:T(8,128)(2,1)S(1)}, u32[]{:S(2)}, u32[]{:S(2)}) async-start(bf16[32,8,256]{2,1,0:T(8,128)(2,1)} %broadcast_in_dim.20), calls=%async_computation | async-start | bytes 262144 | tf_op jit(solution)/shard_map/all_to_all | solution.py:14
  22.0 22.9 %copy-start.2 = (f32[8,256]{1,0:T(8,128)S(1)}, f32[8,256]{1,0:T(8,128)}, u32[]{:S(2)}) copy-start(f32[8,256]{1,0:T(8,128)} %param.12) | copy-start | bytes 24580
  22.0 22.9 %copy-start.3 = (f32[8,256]{1,0:T(8,128)S(1)}, f32[8,256]{1,0:T(8,128)}, u32[]{:S(2)}) copy-start(f32[8,256]{1,0:T(8,128)} %param.10) | copy-start | bytes 24580
  22.1 22.9 %copy-start.4 = (f32[256]{0:T(256)S(1)}, f32[256]{0:T(256)}, u32[]{:S(2)}) copy-start(f32[256]{0:T(256)} %param.13) | copy-start | bytes 3076
  23.4 34.4 %copy-start.7 = (s32[48]{0:T(128)S(1)}, s32[48]{0:T(128)}, u32[]{:S(2)}) copy-start(s32[48]{0:T(128)} %param.17) | copy-start | bytes 580
  45.6 10.7 %all-to-all-start.2 = ((bf16[16,8,256]{2,1,0:T(8,128)(2,1)}), bf16[16,8,256]{2,1,0:T(8,128)(2,1)S(1)}, u32[]{:S(2)}, u32[]{:S(2)}) async-start(bf16[16,8,256]{2,1,0:T(8,128)(2,1)} %broadcast_in_dim.26), calls=%async_computation.2 | async-start | bytes 131072 | tf_op jit(solution)/shard_map/all_to_all | solution.py:14
  56.9 6.1 %copy-start.8 = (s32[256]{0:T(256)S(1)}, s32[256]{0:T(256)}, u32[]{:S(2)}) copy-start(s32[256]{0:T(256)} %param.15) | copy-start | bytes 3076
  56.9 18.1 %copy-start.1 = (f32[8,256]{1,0:T(8,128)S(1)}, f32[8,256]{1,0:T(8,128)}, u32[]{:S(2)}) copy-start(f32[8,256]{1,0:T(8,128)} %param.11) | copy-start | bytes 24580
  56.9 18.1 %copy-start.5 = (f32[256]{0:T(256)S(1)}, f32[256]{0:T(256)}, u32[]{:S(2)}) copy-start(f32[256]{0:T(256)} %param.14) | copy-start | bytes 3076
  59.1 15.9 %all-to-all-start.3 = ((f32[32,8,256]{2,1,0:T(8,128)}), f32[32,8,256]{2,1,0:T(8,128)S(1)}, u32[]{:S(2)}, u32[]{:S(2)}) async-start(f32[32,8,256]{2,1,0:T(8,128)} %bitcast.42), calls=%async_computation.3 | async-start | bytes 524288 | tf_op jit(solution)/shard_map/all_to_all | solution.py:18

commit v2 on v1

--- a/solution.py
+++ b/solution.py
@@ -15,7 +15,8 @@
 
 
 def to_owners(parts, axis):
-    return jnp.sum(lax.all_to_all(parts, axis, 0, 0, tiled=True).astype(jnp.float32), axis=0)
+    got = lax.all_to_all(parts.astype(jnp.bfloat16), axis, 0, 0, tiled=True)
+    return jnp.sum(got.astype(jnp.float32), axis=0)
 
 
 def as_tiles(slabs):

time: 133 us -> 126 us (0.947)
  blocking collectives: 74 us -> 68.7 us
  waiting for transfers between devices: 27.2 us -> 25.6 us
    all_to_all x3, blocking collectives: 50.6 us -> 45.7 us  [to_owners(): got = lax.all_to_all(parts.astype(jnp.bfloat16), axis, 0, 0, tiled=True)]
    all_to_all x1, waiting for transfers between devices: 12 us -> 9.86 us  [to_owners(): got = lax.all_to_all(parts.astype(jnp.bfloat16), axis, 0, 0, tiled=True)]
where the time goes in v2:
time: 126 us
  blocking collectives  68.7 us (55%)
  waiting for transfers between devices  25.6 us (20%)
  starting transfers between devices  17.8 us (14%)
  local copies, waits for them, and re-layouts  4.84 us (4%)
  matrix products  4.09 us (3%)
  other arithmetic  2.93 us (2%)
  between operations  1.58 us (1%)
    all_to_all x3, blocking collectives, to_owners(): got = lax.all_to_all(parts.astype(jnp.bfloat16), axis, 0, 0, tiled=True)  45.7 us
    all_to_all x2, blocking collectives, to_all(): return lax.all_to_all(copies, axis, 0, 0, tiled=True)  23 us
    all_to_all x2, waiting for transfers between devices, to_all(): return lax.all_to_all(copies, axis, 0, 0, tiled=True)  15.8 us
    all_to_all x2, starting transfers between devices, to_all(): return lax.all_to_all(copies, axis, 0, 0, tiled=True)  13.9 us
    all_to_all x1, waiting for transfers between devices, to_owners(): got = lax.all_to_all(parts.astype(jnp.bfloat16), axis, 0, 0, tiled=True)  9.86 us
    all_to_all x1, starting transfers between devices, to_owners(): got = lax.all_to_all(parts.astype(jnp.bfloat16), axis, 0, 0, tiled=True)  3.84 us
  transfers between devices with their start and end apart: 3, of which 3 were waited for; matrix products, arithmetic and copies ran while one was open for 1% of the time, Pallas kernels for 0%

profile of v2, /device:TPU:1, one launch (start us, length us, event | category | flops | bytes accessed | tf_op | source)
XLA Modules:
  0.0 125.6 jit_solution(14707591780722774637)
XLA Ops:
  0.7 0.8 convert_element_type.76
  1.5 0.7 broadcast_in_dim.20
  2.1 10.5 %all-to-all-start = ((bf16[32,8,256]{2,1,0:T(8,128)(2,1)}), bf16[32,8,256]{2,1,0:T(8,128)(2,1)S(1)}, u32[]{:S(2)}, u32[]{:S(2)}) async-start(bf16[32,8,256]{2,1,0:T(8,128)(2,1)} %broadcast_in_dim.20), calls=%async_computation | async-start | bytes 262144 | tf_op jit(solution)/shard_map/all_to_all | solution.py:14
  12.6 0.7 compare_select_fusion.1
  14.0 8.0 %all-to-all-done = bf16[32,8,256]{2,1,0:T(8,128)(2,1)S(1)} async-done(((bf16[32,8,256]{2,1,0:T(8,128)(2,1)}), bf16[32,8,256]{2,1,0:T(8,128)(2,1)S(1)}, u32[]{:S(2)}, u32[]{:S(2)}) %all-to-all-start) | async-done | bytes 131104 | tf_op jit(solution)/shard_map/all_to_all | solution.py:14
  22.0 0.6 gather_fusion
  23.4 20.0 %all_to_all.40 = bf16[16,8,256]{2,1,0:T(8,128)(2,1)S(1)} all-to-all(bf16[16,8,256]{2,1,0:T(8,128)(2,1)S(1)} %bitcast.53), channel_id=1, replica_groups=mesh['row'=16,'col'=32] {'row'}, dimensions={0} | all-to-all | bytes 131072 | tf_op jit(solution)/shard_map/all_to_all | solution.py:18
  43.5 0.6 broadcast_in_dim.26
  44.1 3.4 %all-to-all-start.2 = ((bf16[16,8,256]{2,1,0:T(8,128)(2,1)}), bf16[16,8,256]{2,1,0:T(8,128)(2,1)S(1)}, u32[]{:S(2)}, u32[]{:S(2)}) async-start(bf16[16,8,256]{2,1,0:T(8,128)(2,1)} %broadcast_in_dim.26), calls=%async_computation.2 | async-start | bytes 131072 | tf_op jit(solution)/shard_map/all_to_all | solution.py:14
  47.6 7.8 %all-to-all-done.2 = bf16[16,8,256]{2,1,0:T(8,128)(2,1)S(1)} async-done(((bf16[16,8,256]{2,1,0:T(8,128)(2,1)}), bf16[16,8,256]{2,1,0:T(8,128)(2,1)S(1)}, u32[]{:S(2)}, u32[]{:S(2)}) %all-to-all-start.2) | async-done | bytes 65568 | tf_op jit(solution)/shard_map/all_to_all | solution.py:14
  55.4 0.6 gather_fusion.1
  56.1 0.9 fusion.26
  57.4 0.8 copy.33
  58.2 3.8 %all-to-all-start.3 = ((bf16[32,8,256]{2,1,0:T(8,128)(2,1)}), bf16[32,8,256]{2,1,0:T(8,128)(2,1)S(1)}, u32[]{:S(2)}, u32[]{:S(2)}) async-start(bf16[32,8,256]{2,1,0:T(8,128)(2,1)} %bitcast.42), calls=%async_computation.3 | async-start | bytes 262144 | tf_op jit(solution)/shard_map/all_to_all | solution.py:18
  62.0 9.9 %all-to-all-done.3 = bf16[32,8,256]{2,1,0:T(8,128)(2,1)S(1)} async-done(((bf16[32,8,256]{2,1,0:T(8,128)(2,1)}), bf16[32,8,256]{2,1,0:T(8,128)(2,1)S(1)}, u32[]{:S(2)}, u32[]{:S(2)}) %all-to-all-start.3) | async-done | bytes 131104 | tf_op jit(solution)/shard_map/all_to_all | solution.py:18
  72.0 12.7 %all_to_all.41 = bf16[32,8,256]{2,1,0:T(8,128)(2,1)S(1)} all-to-all(bf16[32,8,256]{2,1,0:T(8,128)(2,1)S(1)} %broadcast_in_dim.28), channel_id=1, replica_groups=mesh['row'=16,'col'=32] {'col'}, dimensions={0} | all-to-all | bytes 262144 | tf_op jit(solution)/shard_map/all_to_all | solution.py:14
  84.7 0.6 gather_fusion.2
  86.1 12.9 %all_to_all.42 = bf16[16,8,256]{2,1,0:T(8,128)(2,1)S(1)} all-to-all(bf16[16,8,256]{2,1,0:T(8,128)(2,1)S(1)} %bitcast.54), channel_id=1, replica_groups=mesh['row'=16,'col'=32] {'row'}, dimensions={0} | all-to-all | bytes 131072 | tf_op jit(solution)/shard_map/all_to_all | solution.py:18
  99.0 0.6 subtract_convert_fusion
  99.6 10.4 %all_to_all.43 = bf16[16,8,256]{2,1,0:T(8,128)(2,1)S(1)} all-to-all(bf16[16,8,256]{2,1,0:T(8,128)(2,1)S(1)} %broadcast_in_dim.29), channel_id=1, replica_groups=mesh['row'=16,'col'=32] {'row'}, dimensions={0} | all-to-all | bytes 131072 | tf_op jit(solution)/shard_map/all_to_all | solution.py:14
  110.0 0.6 gather_fusion.3
  110.6 0.9 fusion.28
  112.1 12.8 %all_to_all.44 = bf16[32,8,256]{2,1,0:T(8,128)(2,1)S(1)} all-to-all(bf16[32,8,256]{2,1,0:T(8,128)(2,1)S(1)} %bitcast.48), channel_id=1, replica_groups=mesh['row'=16,'col'=32] {'col'}, dimensions={0} | all-to-all | bytes 262144 | tf_op jit(solution)/shard_map/all_to_all | solution.py:18
  125.0 0.6 maximum_select_fusion
  (48 shorter events, 2.8 us)
Async XLA Ops:
  0.6 22.0 %copy-start = (bf16[48,128,128]{2,1,0:T(8,128)(2,1)S(1)}, bf16[48,128,128]{2,1,0:T(8,128)(2,1)}, u32[]{:S(2)}) copy-start(bf16[48,128,128]{2,1,0:T(8,128)(2,1)} %param.16) | copy-start | bytes 4718596
  0.6 22.5 %copy-start.6 = (s32[48]{0:T(128)S(1)}, s32[48]{0:T(128)}, u32[]{:S(2)}) copy-start(s32[48]{0:T(128)} %param.18) | copy-start | bytes 580
  2.1 19.9 %all-to-all-start = ((bf16[32,8,256]{2,1,0:T(8,128)(2,1)}), bf16[32,8,256]{2,1,0:T(8,128)(2,1)S(1)}, u32[]{:S(2)}, u32[]{:S(2)}) async-start(bf16[32,8,256]{2,1,0:T(8,128)(2,1)} %broadcast_in_dim.20), calls=%async_computation | async-start | bytes 262144 | tf_op jit(solution)/shard_map/all_to_all | solution.py:14
  14.0 29.5 %copy-start.2 = (f32[8,256]{1,0:T(8,128)S(1)}, f32[8,256]{1,0:T(8,128)}, u32[]{:S(2)}) copy-start(f32[8,256]{1,0:T(8,128)} %param.12) | copy-start | bytes 24580
  14.0 29.5 %copy-start.3 = (f32[8,256]{1,0:T(8,128)S(1)}, f32[8,256]{1,0:T(8,128)}, u32[]{:S(2)}) copy-start(f32[8,256]{1,0:T(8,128)} %param.10) | copy-start | bytes 24580
  14.0 29.5 %copy-start.4 = (f32[256]{0:T(256)S(1)}, f32[256]{0:T(256)}, u32[]{:S(2)}) copy-start(f32[256]{0:T(256)} %param.13) | copy-start | bytes 3076
  23.2 33.8 %copy-start.7 = (s32[48]{0:T(128)S(1)}, s32[48]{0:T(128)}, u32[]{:S(2)}) copy-start(s32[48]{0:T(128)} %param.17) | copy-start | bytes 580
  44.1 11.3 %all-to-all-start.2 = ((bf16[16,8,256]{2,1,0:T(8,128)(2,1)}), bf16[16,8,256]{2,1,0:T(8,128)(2,1)S(1)}, u32[]{:S(2)}, u32[]{:S(2)}) async-start(bf16[16,8,256]{2,1,0:T(8,128)(2,1)} %broadcast_in_dim.26), calls=%async_computation.2 | async-start | bytes 131072 | tf_op jit(solution)/shard_map/all_to_all | solution.py:14
  47.6 14.4 %copy-start.8 = (s32[256]{0:T(256)S(1)}, s32[256]{0:T(256)}, u32[]{:S(2)}) copy-start(s32[256]{0:T(256)} %param.15) | copy-start | bytes 3076
  55.4 16.5 %copy-start.1 = (f32[8,256]{1,0:T(8,128)S(1)}, f32[8,256]{1,0:T(8,128)}, u32[]{:S(2)}) copy-start(f32[8,256]{1,0:T(8,128)} %param.11) | copy-start | bytes 24580
  55.4 16.5 %copy-start.5 = (f32[256]{0:T(256)S(1)}, f32[256]{0:T(256)}, u32[]{:S(2)}) copy-start(f32[256]{0:T(256)} %param.14) | copy-start | bytes 3076
  58.2 13.7 %all-to-all-start.3 = ((bf16[32,8,256]{2,1,0:T(8,128)(2,1)}), bf16[32,8,256]{2,1,0:T(8,128)(2,1)S(1)}, u32[]{:S(2)}, u32[]{:S(2)}) async-start(bf16[32,8,256]{2,1,0:T(8,128)(2,1)} %bitcast.42), calls=%async_computation.3 | async-start | bytes 262144 | tf_op jit(solution)/shard_map/all_to_all | solution.py:18

commit v3 on v1

v3 whole, which is shorter than its diff:
```python
import functools
import math

import jax
import jax.numpy as jnp
from jax import lax
from jax.experimental import pallas as pl
from jax.experimental.pallas import tpu as pltpu
from jax.sharding import Mesh, PartitionSpec as P

ITERS = 2
PRIMAL_STEP = 0.4
DUAL_STEP = 0.4
LANES = 128
CORES = 2
TILE_MAX, UPPER_MAX, DUAL_MAX, RHS_MAX = 0.125, 1.5, 1.0, 6.0
HALF_MAX = 65504.0


def step_down(bound):
    return 2.0 ** min(0, math.floor(math.log2(0.95 * HALF_MAX / bound)))


def to_all(piece, axis):
    copies = jnp.broadcast_to(piece[None], (lax.axis_size(axis), *piece.shape))
    return lax.all_to_all(copies, axis, 0, 0, tiled=True)


def tiles_kernel(contract, from_ref, to_ref, count_ref, source_ref, tiles_ref, out_ref):
    parts = out_ref.shape[-1] // LANES
    source_parts = source_ref.shape[-1] // LANES
    out_ref[...] = jnp.zeros_like(out_ref)
    for slot in range(tiles_ref.shape[0]):
        origin, target = from_ref[slot], to_ref[slot]
        lanes = pl.ds(pl.multiple_of((origin % source_parts) * LANES, LANES), LANES)
        product = lax.dot_general(
            source_ref[origin // source_parts, :, lanes],
            tiles_ref[slot],
            (((1,), (contract,)), ((), ())),
            preferred_element_type=jnp.float32,
        )
        product = jnp.where(slot < count_ref[0], product, 0.0)
        lanes = pl.ds(pl.multiple_of((target % parts) * LANES, LANES), LANES)
        out_ref[target // parts, :, lanes] += product


def tile_products(contract, origin, target, count, source, tiles, slabs):
    smem, vmem = pl.BlockSpec(memory_space=pltpu.SMEM), pl.BlockSpec(memory_space=pltpu.VMEM)
    slots, width, lanes = tiles.shape[0], source.shape[1], source.shape[2]
    return pl.pallas_call(
        functools.partial(tiles_kernel, contract),
        out_shape=jax.ShapeDtypeStruct((slabs, width, lanes), jnp.float32),
        in_specs=[smem, smem, smem, vmem, vmem],
        out_specs=vmem,
        cost_estimate=pl.CostEstimate(
            flops=2 * slots * width * LANES * LANES, bytes_accessed=tiles.size * 2, transcendentals=0
        ),
        compiler_params=pltpu.CompilerParams(vmem_limit_bytes=16 * 2**20),
    )(origin, target, count, source, tiles)


def split(value):
    high = lax.reduce_precision(value, 5, 10)
    return high.astype(jnp.float16), (value - high).astype(jnp.float16)


def body(primal, dual, cost, upper, rhs, row_kind, tiles, tile_rows, tile_cols, tile_count):
    planes = lax.axis_size("z")
    col_devices = lax.axis_size("col")
    slots, width, piece = tiles.shape[0], primal.shape[0], primal.shape[1]
    per_piece = piece // LANES
    col_tiles = per_piece * planes * CORES
    row_tiles = per_piece * col_devices
    core = lax.axis_index("core")
    owner = tile_cols // per_piece
    tile_at = ((owner % CORES) * planes + owner // CORES) * per_piece + tile_cols % per_piece

    limits = jnp.pad(jnp.stack(split(upper)), ((0, width - 2), (0, 0)))
    state = lax.optimization_barrier(jnp.stack([*split(primal), *split(cost), limits]))

    y = dual
    y_max = DUAL_MAX
    x_half = None
    for _ in range(ITERS):
        y_rows = to_all(y.astype(jnp.bfloat16), "col")
        partial_grad = tile_products(0, tile_rows, tile_at, tile_count, y_rows, tiles, CORES * planes)

        both = lax.all_gather(partial_grad, "core", axis=0).reshape(CORES, CORES, planes, width, piece)
        mine = jnp.sum(lax.dynamic_index_in_dim(both, core, 1, keepdims=False), axis=0)
        scale = step_down(CORES * min(slots, row_tiles) * LANES * TILE_MAX * y_max)
        sends = (mine * scale).astype(jnp.float16)
        if x_half is None:
            sends = jnp.concatenate([sends, state])
        got = to_all(sends, "z")
        grad = jnp.sum(got[:, :planes].astype(jnp.float32), axis=0) * (1.0 / scale)
        if x_half is None:
            x_half = got[:, planes].astype(jnp.float32) + got[:, planes + 1].astype(jnp.float32)
            cost_half = got[:, planes + 2].astype(jnp.float32) + got[:, planes + 3].astype(jnp.float32)
            bounds = got[:, planes + 4].astype(jnp.float32)
            upper_half = bounds[:, 0:1] + bounds[:, 1:2]

        x_new = jnp.clip(x_half - PRIMAL_STEP * (cost_half - grad), 0.0, upper_half)
        xbar = (2.0 * x_new - x_half).astype(jnp.bfloat16)
        x_cols = lax.all_gather(xbar, "core", axis=0, tiled=True)
        partial_image = tile_products(1, tile_at, tile_rows, tile_count, x_cols, tiles, col_devices)
        h_max = min(slots, col_tiles) * LANES * TILE_MAX * 2 * UPPER_MAX
        scale = step_down(h_max)
        got = lax.all_to_all((partial_image * scale).astype(jnp.float16), "col", 0, 0, tiled=True)
        image = jnp.sum(got.astype(jnp.float32), axis=0) * (1.0 / scale)
        y_new = y + DUAL_STEP * (rhs[None, :] - image)
        y = jnp.where(row_kind[None, :] == 1, jnp.maximum(y_new, 0.0), y_new)
        y_max = y_max + DUAL_STEP * (RHS_MAX + col_devices * h_max)
        x_half = x_new
    return lax.dynamic_index_in_dim(x_half, lax.axis_index("z"), 0, keepdims=False), y


def solution(mesh):
    rows, cols = mesh.devices.shape
    split_mesh = Mesh(mesh.devices.reshape(rows // CORES, CORES, cols), ("z", "core", "col"))
    by_col, by_row = ("col", "z", "core"), ("z", "core", "col")
    in_specs = (
        P(None, by_col),
        P(None, by_row),
        P(None, by_col),
        P(by_col),
        P(by_row),
        P(by_row),
        P(by_row, None, None),
        P(by_row),
        P(by_row),
        P(by_row),
    )
    out_specs = (P(None, by_col), P(None, by_row))
    return jax.shard_map(body, mesh=split_mesh, in_specs=in_specs, out_specs=out_specs, check_vma=False)
```

time: 133 us -> 126 us (0.947)
  blocking collectives: 74 us -> 65.8 us
  Pallas kernels: 0 us -> 5.58 us
  other arithmetic: 2.93 us -> 7.16 us
  waiting for transfers between devices: 27.2 us -> 23 us
  matrix products: 4.08 us -> 0 us
  local copies, waits for them, and re-layouts: 5 us -> 3.43 us
    all_to_all x3 -> x0, blocking collectives: 50.6 us -> none  [to_owners(): lax.all_to_all(parts, axis, 0, 0, tiled=True).astype(jnp.float32)]
    all_to_all x2 -> x3, blocking collectives: 23.4 us -> 52.2 us  [to_all(): return lax.all_to_all(copies, axis, 0, 0, tiled=True)]
    all_gather x0 -> x4, blocking collectives: none -> 13.5 us  [the longest x2 8.32 us: body(): lax.all_gather(partial_grad, 'core', axis=0)]
    all_to_all x2 -> x1, waiting for transfers between devices: 15.3 us -> 4.44 us  [to_all(): return lax.all_to_all(copies, axis, 0, 0, tiled=True)]
    all_to_all x1 -> x2, waiting for transfers between devices: 12 us -> 18.6 us  [body(): lax.all_to_all((partial_image * scale).astype(jnp.float16), 'col', 0, 0,...]
    pallas_call x0 -> x4, Pallas kernels: none -> 5.58 us  [tile_products(): pl.pallas_call(functools.partial(tiles_kernel, contract), out_shape=jax.S...]
    dot_general x8 -> x0, matrix products: 4.08 us -> none  [the longest x2 1.81 us: body(): jnp.einsum('trk,tjk->trj', x_cols[tile_cols], tiles, preferred_element_ty...]
    all_to_all x1 -> x2, starting transfers between devices: 3.87 us -> 7.82 us  [body(): lax.all_to_all((partial_image * scale).astype(jnp.float16), 'col', 0, 0,...]
  transfers between devices with their start and end apart: 3 -> 3, of which waited for: 3 -> 3; matrix products, arithmetic and copies ran while one was open for 1% -> 4% of each run, Pallas kernels for 0% -> 0%
where the time goes in v3:
time: 126 us; the launch traced here: 125 us
  blocking collectives  65.8 us (52%)
  waiting for transfers between devices  23 us (18%)
  starting transfers between devices  18.3 us (15%)
  other arithmetic  7.16 us (6%)
  Pallas kernels  5.58 us (4%)
  local copies, waits for them, and re-layouts  3.43 us (3%)
  between operations  1.47 us (1%)
    all_to_all x3, blocking collectives, to_all(): return lax.all_to_all(copies, axis, 0, 0, tiled=True)  52.2 us
    all_to_all x2, waiting for transfers between devices, body(): lax.all_to_all((partial_image * scale).astype(jnp.float16), 'col', 0, 0,...  18.6 us
    all_to_all x1, starting transfers between devices, to_all(): return lax.all_to_all(copies, axis, 0, 0, tiled=True)  10.5 us
    all_gather x2, blocking collectives, body(): lax.all_gather(partial_grad, 'core', axis=0)  8.32 us
    all_to_all x2, starting transfers between devices, body(): lax.all_to_all((partial_image * scale).astype(jnp.float16), 'col', 0, 0,...  7.82 us
    pallas_call x4, Pallas kernels, tile_products(): pl.pallas_call(functools.partial(tiles_kernel, contract), out_shape=jax.S...  5.58 us
    all_gather x2, blocking collectives, body(): x_cols = lax.all_gather(xbar, 'core', axis=0, tiled=True)  5.23 us
    all_to_all x1, waiting for transfers between devices, to_all(): return lax.all_to_all(copies, axis, 0, 0, tiled=True)  4.44 us
  transfers between devices with their start and end apart: 3, of which 3 were waited for; matrix products, arithmetic and copies ran while one was open for 4% of the time, Pallas kernels for 0%

profile of v3, /device:TPU:1, one launch (start us, length us, event | category | flops | bytes accessed | tf_op | source)
XLA Modules:
  0.0 124.8 jit_solution(1635503070631089004)
XLA Ops:
  0.6 0.7 convert_element_type.82
  2.0 10.5 %all-to-all-start = ((bf16[32,8,256]{2,1,0:T(8,128)(2,1)}), bf16[32,8,256]{2,1,0:T(8,128)(2,1)S(1)}, u32[]{:S(2)}, u32[]{:S(2)}) async-start(bf16[32,8,256]{2,1,0:T(8,128)(2,1)} %broadcast_in_dim.19), calls=%async_computation | async-start | bytes 262144 | tf_op jit(solution)/shard_map/all_to_all | solution.py:26
  12.5 0.7 reduce-precision_convert_fusion.2
  13.2 0.7 constant_dynamic-update-slice_fusion.4
  13.9 0.7 constant_dynamic-update-slice_fusion.3
  14.6 0.7 constant_dynamic-update-slice_fusion.2
  15.3 0.7 constant_dynamic-update-slice_fusion.1
  17.4 4.4 %all-to-all-done.source_ref = bf16[32,8,256]{2,1,0:T(8,128)(2,1)S(1)} async-done(((bf16[32,8,256]{2,1,0:T(8,128)(2,1)}), bf16[32,8,256]{2,1,0:T(8,128)(2,1)S(1)}, u32[]{:S(2)}, u32[]{:S(2)}) %all-to-all-start) | async-done | bytes 131104 | tf_op jit(solution)/shard_map/all_to_all | solution.py:26
  21.8 1.4 %copy-done = bf16[48,128,128]{2,1,0:T(8,128)(2,1)S(1)} copy-done((bf16[48,128,128]{2,1,0:T(8,128)(2,1)S(1)}, bf16[48,128,128]{2,1,0:T(8,128)(2,1)}, u32[]{:S(2)}) %copy-start) | copy-done | bytes 1572888
  23.9 1.3 %shard_map.113 = f32[16,8,256]{2,1,0:T(8,128)S(1)} custom-call(s32[48]{0:T(128)S(1)} %copy-done.2, s32[48]{0:T(128)S(1)} %fusion.22.to_ref.from_ref, s32[1]{0:T(128)S(6)} %copy.29.count_ref, bf16[32,8,256]{2,1,0:T(8,128)(2,1)S(1)} %all-to-all-done.source_ref, bf16[48,128,128]{2,1,0:T(8,128)(2,1)S(1)} %copy-done), custom_call_target="tpu_custom_call" | custom-call | flops 12582912 | bytes 1572864 | tf_op jit(solution)/shard_map/pallas_call | solution.py:50
  25.2 3.8 %all-gather = f32[32,8,256]{2,1,0:T(8,128)S(1)} all-gather(f32[16,8,256]{2,1,0:T(8,128)S(1)} %shard_map.113), channel_id=2, replica_groups=mesh['z'=8,'core'=2,'col'=32] {'core'}, dimensions={0}, use_global_device_ids=true | all-gather | bytes 393216 | tf_op jit(solution)/shard_map/all_gather | solution.py:88
  29.1 24.4 %all_to_all.30 = f16[8,13,8,256]{3,2,1,0:T(8,128)(2,1)S(1)} all-to-all(f16[8,13,8,256]{3,2,1,0:T(8,128)(2,1)S(1)} %broadcast_in_dim.20), channel_id=1, replica_groups=mesh['z'=8,'core'=2,'col'=32] {'z'}, dimensions={0} | all-to-all | bytes 851968 | tf_op jit(solution)/shard_map/all_to_all | solution.py:26
  53.7 3.2 %all_gather.20.source_ref = bf16[16,8,256]{2,1,0:T(8,128)(2,1)S(1)} all-gather(bf16[8,8,256]{2,1,0:T(8,128)(2,1)S(1)} %get-tuple-element.4), channel_id=1, replica_groups=mesh['z'=8,'core'=2,'col'=32] {'core'}, dimensions={0}, use_global_device_ids=true | all-gather | bytes 98304 | tf_op jit(solution)/shard_map/all_gather | solution.py:104
  57.0 1.5 %shard_map.114 = f32[32,8,256]{2,1,0:T(8,128)S(1)} custom-call(s32[48]{0:T(128)S(1)} %fusion.22.to_ref.from_ref, s32[48]{0:T(128)S(1)} %copy-done.2, s32[1]{0:T(128)S(6)} %copy.29.count_ref, bf16[16,8,256]{2,1,0:T(8,128)(2,1)S(1)} %all_gather.20.source_ref, bf16[48,128,128]{2,1,0:T(8,128)(2,1)S(1)} %copy-done.1), custom_call_target="tpu_custom_call" | custom-call | flops 12582912 | bytes 1572864 | tf_op jit(solution)/shard_map/pallas_call | solution.py:50
  59.1 4.0 %all-to-all-start.2 = ((f16[32,8,256]{2,1,0:T(8,128)(2,1)}), f16[32,8,256]{2,1,0:T(8,128)(2,1)S(1)}, u32[]{:S(2)}, u32[]{:S(2)}) async-start(f16[32,8,256]{2,1,0:T(8,128)(2,1)} %convert_element_type.98), calls=%async_computation.2 | async-start | bytes 262144 | tf_op jit(solution)/shard_map/all_to_all | solution.py:108
  63.1 9.3 %all-to-all-done.2 = f16[32,8,256]{2,1,0:T(8,128)(2,1)S(1)} async-done(((f16[32,8,256]{2,1,0:T(8,128)(2,1)}), f16[32,8,256]{2,1,0:T(8,128)(2,1)S(1)}, u32[]{:S(2)}, u32[]{:S(2)}) %all-to-all-start.2) | async-done | bytes 131104 | tf_op jit(solution)/shard_map/all_to_all | solution.py:108
  72.5 13.0 %all_to_all.31.source_ref = bf16[32,8,256]{2,1,0:T(8,128)(2,1)S(1)} all-to-all(bf16[32,8,256]{2,1,0:T(8,128)(2,1)S(1)} %broadcast_in_dim.22), channel_id=1, replica_groups=mesh['z'=8,'core'=2,'col'=32] {'col'}, dimensions={0} | all-to-all | bytes 262144 | tf_op jit(solution)/shard_map/all_to_all | solution.py:26
  85.6 1.3 %shard_map.115 = f32[16,8,256]{2,1,0:T(8,128)S(1)} custom-call(s32[48]{0:T(128)S(1)} %copy-done.3, s32[48]{0:T(128)S(1)} %fusion.22.to_ref.from_ref, s32[1]{0:T(128)S(6)} %copy.29.count_ref, bf16[32,8,256]{2,1,0:T(8,128)(2,1)S(1)} %all_to_all.31.source_ref, bf16[48,128,128]{2,1,0:T(8,128)(2,1)S(1)} %copy-done.1), custom_call_target="tpu_custom_call" | custom-call | flops 12582912 | bytes 1572864 | tf_op jit(solution)/shard_map/pallas_call | solution.py:50
  86.9 4.5 %all-gather.1 = f32[32,8,256]{2,1,0:T(8,128)S(1)} all-gather(f32[16,8,256]{2,1,0:T(8,128)S(1)} %shard_map.115), channel_id=3, replica_groups=mesh['z'=8,'core'=2,'col'=32] {'core'}, dimensions={0}, use_global_device_ids=true | all-gather | bytes 393216 | tf_op jit(solution)/shard_map/all_gather | solution.py:88
  91.4 14.8 %all_to_all.32 = f16[8,8,8,256]{3,2,1,0:T(8,128)(2,1)S(1)} all-to-all(f16[8,8,8,256]{3,2,1,0:T(8,128)(2,1)S(1)} %broadcast_in_dim.23), channel_id=1, replica_groups=mesh['z'=8,'core'=2,'col'=32] {'z'}, dimensions={0} | all-to-all | bytes 524288 | tf_op jit(solution)/shard_map/all_to_all | solution.py:26
  106.3 2.0 %all_gather.23.source_ref = bf16[16,8,256]{2,1,0:T(8,128)(2,1)S(1)} all-gather(bf16[8,8,256]{2,1,0:T(8,128)(2,1)S(1)} %get-tuple-element.2), channel_id=1, replica_groups=mesh['z'=8,'core'=2,'col'=32] {'core'}, dimensions={0}, use_global_device_ids=true | all-gather | bytes 98304 | tf_op jit(solution)/shard_map/all_gather | solution.py:104
  108.2 1.5 %shard_map.116 = f32[32,8,256]{2,1,0:T(8,128)S(1)} custom-call(s32[48]{0:T(128)S(1)} %fusion.22.to_ref.from_ref, s32[48]{0:T(128)S(1)} %copy-done.3, s32[1]{0:T(128)S(6)} %copy.29.count_ref, bf16[16,8,256]{2,1,0:T(8,128)(2,1)S(1)} %all_gather.23.source_ref, bf16[48,128,128]{2,1,0:T(8,128)(2,1)S(1)} %copy-done.1), custom_call_target="tpu_custom_call" | custom-call | flops 12582912 | bytes 1572864 | tf_op jit(solution)/shard_map/pallas_call | solution.py:50
  110.4 3.9 %all-to-all-start.5 = ((f16[32,8,256]{2,1,0:T(8,128)(2,1)}), f16[32,8,256]{2,1,0:T(8,128)(2,1)S(1)}, u32[]{:S(2)}, u32[]{:S(2)}) async-start(f16[32,8,256]{2,1,0:T(8,128)(2,1)} %convert_element_type.104), calls=%async_computation.5 | async-start | bytes 262144 | tf_op jit(solution)/shard_map/all_to_all | solution.py:108
  114.9 9.3 %all-to-all-done.5 = f16[32,8,256]{2,1,0:T(8,128)(2,1)S(1)} async-done(((f16[32,8,256]{2,1,0:T(8,128)(2,1)}), f16[32,8,256]{2,1,0:T(8,128)(2,1)S(1)}, u32[]{:S(2)}, u32[]{:S(2)}) %all-to-all-start.5) | async-done | bytes 131104 | tf_op jit(solution)/shard_map/all_to_all | solution.py:108
  (41 shorter events, 4.9 us)
Async XLA Ops:
  2.0 19.9 %all-to-all-start = ((bf16[32,8,256]{2,1,0:T(8,128)(2,1)}), bf16[32,8,256]{2,1,0:T(8,128)(2,1)S(1)}, u32[]{:S(2)}, u32[]{:S(2)}) async-start(bf16[32,8,256]{2,1,0:T(8,128)(2,1)} %broadcast_in_dim.19), calls=%async_computation | async-start | bytes 262144 | tf_op jit(solution)/shard_map/all_to_all | solution.py:26
  21.8 1.4 %copy-start = (bf16[48,128,128]{2,1,0:T(8,128)(2,1)S(1)}, bf16[48,128,128]{2,1,0:T(8,128)(2,1)}, u32[]{:S(2)}) copy-start(bf16[48,128,128]{2,1,0:T(8,128)(2,1)} %tiles_ref.7) | copy-start | bytes 4718596
  23.2 0.7 copy-start.2
  25.2 31.8 %copy-start.1 = (bf16[48,128,128]{2,1,0:T(8,128)(2,1)S(1)}, bf16[48,128,128]{2,1,0:T(8,128)(2,1)}, u32[]{:S(2)}) copy-start(bf16[48,128,128]{2,1,0:T(8,128)(2,1)} %tiles_ref.7) | copy-start | bytes 4718596
  53.6 9.5 %copy-start.6 = (s32[256]{0:T(256)S(1)}, s32[256]{0:T(256)}, u32[]{:S(2)}) copy-start(s32[256]{0:T(256)} %param.15) | copy-start | bytes 3076
  53.6 18.8 %copy-start.4 = (f32[8,256]{1,0:T(8,128)S(1)}, f32[8,256]{1,0:T(8,128)}, u32[]{:S(2)}) copy-start(f32[8,256]{1,0:T(8,128)} %param.11) | copy-start | bytes 24580
  53.7 18.8 %copy-start.5 = (f32[256]{0:T(256)S(1)}, f32[256]{0:T(256)}, u32[]{:S(2)}) copy-start(f32[256]{0:T(256)} %param.14) | copy-start | bytes 3076
  57.0 28.6 %copy-start.3 = (s32[48]{0:T(128)S(1)}, s32[48]{0:T(128)}, u32[]{:S(2)}) copy-start(s32[48]{0:T(128)} %to_ref.3) | copy-start | bytes 580
  59.1 13.3 %all-to-all-start.2 = ((f16[32,8,256]{2,1,0:T(8,128)(2,1)}), f16[32,8,256]{2,1,0:T(8,128)(2,1)S(1)}, u32[]{:S(2)}, u32[]{:S(2)}) async-start(f16[32,8,256]{2,1,0:T(8,128)(2,1)} %convert_element_type.98), calls=%async_computation.2 | async-start | bytes 262144 | tf_op jit(solution)/shard_map/all_to_all | solution.py:108
  110.4 13.7 %all-to-all-start.5 = ((f16[32,8,256]{2,1,0:T(8,128)(2,1)}), f16[32,8,256]{2,1,0:T(8,128)(2,1)S(1)}, u32[]{:S(2)}, u32[]{:S(2)}) async-start(f16[32,8,256]{2,1,0:T(8,128)(2,1)} %convert_element_type.104), calls=%async_computation.5 | async-start | bytes 262144 | tf_op jit(solution)/shard_map/all_to_all | solution.py:108

commit v4 on v3

v4 whole, which is shorter than its diff:
```python
import functools
import math

import jax
import jax.numpy as jnp
from jax import lax
from jax.experimental import pallas as pl
from jax.experimental.pallas import tpu as pltpu
from jax.sharding import Mesh, PartitionSpec as P

ITERS = 2
PRIMAL_STEP = 0.4
DUAL_STEP = 0.4
LANES = 128
CORES = 2
TILE_MAX, UPPER_MAX, DUAL_MAX, RHS_MAX = 0.125, 1.5, 1.0, 6.0
HALF_MAX = 65504.0
ROW_AT, COL_AT, PLANE = range(3)


def step_down(bound):
    return 2.0 ** min(0, math.floor(math.log2(0.95 * HALF_MAX / bound)))


def to_all(piece, axis, dtype):
    copies = jnp.broadcast_to(piece[None], (lax.axis_size(axis), *piece.shape)).astype(dtype)
    return lax.all_to_all(copies, axis, 0, 0, tiled=True)


def tiles_kernel(contract, origins, targets, index_ref, source_ref, tiles_ref, *refs):
    state_ref, out_ref, own_ref, products_ref = refs if len(refs) == 4 else (None, refs[0], None, refs[1])
    parts = out_ref.shape[-1] // LANES
    source_parts = source_ref.shape[-1] // LANES
    if state_ref is not None:
        own_ref[...] = state_ref[index_ref[PLANE, 0]]
    out_ref[...] = jnp.zeros_like(out_ref)
    slots = tiles_ref.shape[0]
    for slot in range(slots):
        origin = index_ref[origins, slot]
        lanes = pl.ds(pl.multiple_of((origin % source_parts) * LANES, LANES), LANES)
        products_ref[slot] = lax.dot_general(
            source_ref[origin // source_parts, :, lanes],
            tiles_ref[slot],
            (((1,), (contract,)), ((), ())),
            preferred_element_type=jnp.float32,
        )
    for slot in range(slots):
        target = index_ref[targets, slot]
        lanes = pl.ds(pl.multiple_of((target % parts) * LANES, LANES), LANES)
        out_ref[target // parts, :, lanes] += products_ref[slot]


def tile_products(contract, origins, targets, index, source, tiles, slabs, state=None):
    smem, vmem = pl.BlockSpec(memory_space=pltpu.SMEM), pl.BlockSpec(memory_space=pltpu.VMEM)
    slots, width, lanes = tiles.shape[0], source.shape[1], source.shape[2]
    out = jax.ShapeDtypeStruct((slabs, width, lanes), jnp.float32)
    own = jax.ShapeDtypeStruct((width, lanes), jnp.float32)
    extra = () if state is None else (state,)
    return pl.pallas_call(
        functools.partial(tiles_kernel, contract, origins, targets),
        out_shape=out if state is None else (out, own),
        in_specs=[smem, vmem, vmem] + [vmem] * len(extra),
        out_specs=vmem if state is None else (vmem, vmem),
        scratch_shapes=[pltpu.VMEM((slots, width, LANES), jnp.float32)],
        cost_estimate=pl.CostEstimate(
            flops=2 * slots * width * LANES * LANES, bytes_accessed=tiles.size * 2, transcendentals=0
        ),
        compiler_params=pltpu.CompilerParams(vmem_limit_bytes=16 * 2**20),
    )(index, source, tiles, *extra)


def split(value):
    high = lax.reduce_precision(value, 5, 10)
    return high.astype(jnp.float16), (value - high).astype(jnp.float16)


def body(primal, dual, cost, upper, rhs, row_kind, tiles, tile_rows, tile_cols, tile_count):
    planes = lax.axis_size("z")
    col_devices = lax.axis_size("col")
    slots, width, piece = tiles.shape[0], primal.shape[0], primal.shape[1]
    per_piece = piece // LANES
    col_tiles = per_piece * planes * CORES
    row_tiles = per_piece * col_devices
    core = lax.axis_index("core")
    owner = tile_cols // per_piece
    tile_at = ((owner % CORES) * planes + owner // CORES) * per_piece + tile_cols % per_piece

    index = jnp.stack([tile_rows, tile_at, jnp.full_like(tile_rows, lax.axis_index("z"))])
    live = jnp.arange(slots, dtype=jnp.int32) < tile_count[0]
    tiles = jnp.where(live[:, None, None], tiles, jnp.zeros_like(tiles))

    limits = jnp.pad(jnp.stack(split(upper)), ((0, width - 2), (0, 0)))
    state = lax.optimization_barrier(jnp.stack([*split(primal), *split(cost), limits]))

    pull = jnp.broadcast_to(DUAL_STEP * rhs[None, :], dual.shape)
    floor = jnp.broadcast_to(jnp.where(row_kind == 1, 0.0, jnp.finfo(jnp.float32).min)[None, :], dual.shape)
    lifted = lax.optimization_barrier(dual) + pull
    y_sends = dual
    y_max = DUAL_MAX
    x_half = None
    for step in range(ITERS):
        y_rows = to_all(y_sends, "col", jnp.bfloat16)
        if step == 0:
            y_rows, index, tiles, state, lifted, pull, floor = lax.optimization_barrier(
                (y_rows, index, tiles, state, lifted, pull, floor)
            )
        partial_grad = tile_products(0, ROW_AT, COL_AT, index, y_rows, tiles, CORES * planes)

        both = lax.all_gather(partial_grad, "core", axis=0).reshape(CORES, CORES, planes, width, piece)
        mine = jnp.sum(lax.dynamic_index_in_dim(both, core, 1, keepdims=False), axis=0)
        scale = step_down(CORES * min(slots, row_tiles) * LANES * TILE_MAX * y_max)
        sends = (mine * scale).astype(jnp.float16)
        if step == 0:
            sends = jnp.concatenate([sends, state])
        got = to_all(sends, "z", jnp.float16)
        grad = jnp.sum(got[:, :planes].astype(jnp.float32), axis=0) * (1.0 / scale)
        if step == 0:
            x_half = got[:, planes].astype(jnp.float32) + got[:, planes + 1].astype(jnp.float32)
            cost_half = got[:, planes + 2].astype(jnp.float32) + got[:, planes + 3].astype(jnp.float32)
            bounds = got[:, planes + 4].astype(jnp.float32)
            upper_half = bounds[:, 0:1] + bounds[:, 1:2]

        x_new = jnp.clip(x_half - PRIMAL_STEP * (cost_half - grad), 0.0, upper_half)
        xbar = (2.0 * x_new - x_half).astype(jnp.bfloat16)
        x_cols = lax.all_gather(xbar, "core", axis=0, tiled=True)
        last = step == ITERS - 1
        partial_image = tile_products(1, COL_AT, ROW_AT, index, x_cols, tiles, col_devices, x_new if last else None)
        if last:
            partial_image, primal_out = partial_image
        h_max = min(slots, col_tiles) * LANES * TILE_MAX * 2 * UPPER_MAX
        scale = step_down(h_max)
        got = lax.all_to_all((partial_image * scale).astype(jnp.float16), "col", 0, 0, tiled=True)
        image = jnp.sum(got.astype(jnp.float32), axis=0)
        y = jnp.maximum(lifted - (DUAL_STEP / scale) * image, floor)
        y_max = y_max + DUAL_STEP * (RHS_MAX + col_devices * h_max)
        y_sends, lifted, x_half = y, y + pull, x_new
    return primal_out, y


def solution(mesh):
    rows, cols = mesh.devices.shape
    split_mesh = Mesh(mesh.devices.reshape(rows // CORES, CORES, cols), ("z", "core", "col"))
    by_col, by_row = ("col", "z", "core"), ("z", "core", "col")
    in_specs = (
        P(None, by_col),
        P(None, by_row),
        P(None, by_col),
        P(by_col),
        P(by_row),
        P(by_row),
        P(by_row, None, None),
        P(by_row),
        P(by_row),
        P(by_row),
    )
    out_specs = (P(None, by_col), P(None, by_row))
    return jax.shard_map(body, mesh=split_mesh, in_specs=in_specs, out_specs=out_specs, check_vma=False)
```

time: 126 us -> 124 us (0.984)
  blocking collectives: 65.8 us -> 94.3 us
  waiting for transfers between devices: 23 us -> 1.27 us
  starting transfers between devices: 18.3 us -> 10.5 us
  local copies, waits for them, and re-layouts: 3.43 us -> 0.82 us
  other arithmetic: 7.16 us -> 8.93 us
    all_to_all x0 -> x2, blocking collectives: none -> 28.6 us  [body(): lax.all_to_all((partial_image * scale).astype(jnp.float16), 'col', 0, 0,...]
    all_to_all x2 -> x0, waiting for transfers between devices: 18.6 us -> none  [body(): lax.all_to_all((partial_image * scale).astype(jnp.float16), 'col', 0, 0,...]
    all_to_all x2 -> x0, starting transfers between devices: 7.82 us -> none  [body(): lax.all_to_all((partial_image * scale).astype(jnp.float16), 'col', 0, 0,...]
    all_to_all x1, waiting for transfers between devices: 4.44 us -> 1.27 us  [to_all(): return lax.all_to_all(copies, axis, 0, 0, tiled=True)]
    unnamed x15 -> x5, local copies, waits for them, and re-layouts: 2.09 us -> 0.01 us
    select_n x1 -> x2, other arithmetic: 0.61 us -> 2.29 us  [the longest x1 1.61 us: body(): tiles = jnp.where(live[:, None, None], tiles, jnp.zeros_like(tiles))]
    convert_element_type x2, other arithmetic: 1.31 us -> 0.04 us  [body(): (partial_image * scale).astype(jnp.float16)]
  transfers between devices with their start and end apart: 3 -> 1, of which waited for: 3 -> 1; matrix products, arithmetic and copies ran while one was open for 4% -> 6% of each run, Pallas kernels for 0% -> 0%
where the time goes in v4:
time: 124 us; the launch traced here: 123 us
  blocking collectives  94.3 us (76%)
  starting transfers between devices  10.5 us (8%)
  other arithmetic  8.93 us (7%)
  Pallas kernels  5.97 us (5%)
  between operations  1.44 us (1%)
  waiting for transfers between devices  1.27 us (1%)
    all_to_all x3, blocking collectives, to_all(): return lax.all_to_all(copies, axis, 0, 0, tiled=True)  52.2 us
    all_to_all x2, blocking collectives, body(): lax.all_to_all((partial_image * scale).astype(jnp.float16), 'col', 0, 0,...  28.6 us
    all_to_all x1, starting transfers between devices, to_all(): return lax.all_to_all(copies, axis, 0, 0, tiled=True)  10.5 us
    all_gather x2, blocking collectives, body(): lax.all_gather(partial_grad, 'core', axis=0)  8.19 us
    pallas_call x4, Pallas kernels, tile_products(): pl.pallas_call(functools.partial(tiles_kernel, contract, origins, targets...  5.97 us
    all_gather x2, blocking collectives, body(): x_cols = lax.all_gather(xbar, 'core', axis=0, tiled=True)  5.23 us
    unnamed x4, other arithmetic  2.84 us
  transfers between devices with their start and end apart: 1, of which 1 were waited for; matrix products, arithmetic and copies ran while one was open for 6% of the time, Pallas kernels for 0%

profile of v4, /device:TPU:1, one launch (start us, length us, event | category | flops | bytes accessed | tf_op | source)
XLA Modules:
  0.0 123.2 jit_solution(10243210974849713258)
XLA Ops:
  0.6 0.7 convert_element_type.84
  2.0 10.5 %all-to-all-start = ((bf16[32,8,256]{2,1,0:T(8,128)(2,1)}), bf16[32,8,256]{2,1,0:T(8,128)(2,1)S(1)}, u32[]{:S(2)}, u32[]{:S(2)}) async-start(bf16[32,8,256]{2,1,0:T(8,128)(2,1)} %broadcast_in_dim.30), calls=%async_computation | async-start | bytes 262144 | tf_op jit(solution)/shard_map/all_to_all | solution.py:27
  13.8 0.7 broadcast_multiply_fusion
  14.5 0.7 compare_select_fusion
  15.2 0.7 reduce-precision_convert_fusion.2
  15.9 0.7 constant_dynamic-update-slice_fusion.4
  16.6 0.7 constant_dynamic-update-slice_fusion.3
  17.3 0.7 constant_dynamic-update-slice_fusion.2
  18.0 0.7 constant_dynamic-update-slice_fusion.1
  18.8 1.6 %broadcast_select_fusion.tiles_ref = bf16[48,128,128]{2,1,0:T(8,128)(2,1)S(1)} fusion(bf16[48,128,128]{2,1,0:T(8,128)(2,1)} %param.16, pred[48]{0:T(512)(128)(4,1)S(1)} %iota_compare_fusion.1), kind=kLoop, calls=%fused_computation | loop fusion | flops 786432 | bytes 3145776 | tf_op jit(solution)/shard_map/jit(_where)/select_n | solution.py:90
  20.6 1.3 %all-to-all-done.source_ref = bf16[32,8,256]{2,1,0:T(8,128)(2,1)S(1)} async-done(((bf16[32,8,256]{2,1,0:T(8,128)(2,1)}), bf16[32,8,256]{2,1,0:T(8,128)(2,1)S(1)}, u32[]{:S(2)}, u32[]{:S(2)}) %all-to-all-start) | async-done | bytes 131104 | tf_op jit(solution)/shard_map/all_to_all | solution.py:27
  21.8 1.3 %shard_map.113 = f32[16,8,256]{2,1,0:T(8,128)S(1)} custom-call(s32[3,48]{1,0:T(4,128)S(1)} %add_add_fusion.index_ref, bf16[32,8,256]{2,1,0:T(8,128)(2,1)S(1)} %all-to-all-done.source_ref, bf16[48,128,128]{2,1,0:T(8,128)(2,1)S(1)} %broadcast_select_fusion.tiles_ref), custom_call_target="tpu_custom_call" | custom-call | flops 12582912 | bytes 1572864 | tf_op jit(solution)/shard_map/pallas_call | solution.py:59
  23.1 3.7 %all-gather = f32[32,8,256]{2,1,0:T(8,128)S(1)} all-gather(f32[16,8,256]{2,1,0:T(8,128)S(1)} %shard_map.113), channel_id=2, replica_groups=mesh['z'=8,'core'=2,'col'=32] {'core'}, dimensions={0}, use_global_device_ids=true | all-gather | bytes 393216 | tf_op jit(solution)/shard_map/all_gather | solution.py:109
  26.9 24.4 %all_to_all.30 = f16[8,13,8,256]{3,2,1,0:T(8,128)(2,1)S(1)} all-to-all(f16[8,13,8,256]{3,2,1,0:T(8,128)(2,1)S(1)} %broadcast_in_dim.63), channel_id=1, replica_groups=mesh['z'=8,'core'=2,'col'=32] {'z'}, dimensions={0} | all-to-all | bytes 851968 | tf_op jit(solution)/shard_map/all_to_all | solution.py:27
  51.4 3.2 %all_gather.20.source_ref = bf16[16,8,256]{2,1,0:T(8,128)(2,1)S(1)} all-gather(bf16[8,8,256]{2,1,0:T(8,128)(2,1)S(1)} %get-tuple-element.22), channel_id=1, replica_groups=mesh['z'=8,'core'=2,'col'=32] {'core'}, dimensions={0}, use_global_device_ids=true | all-gather | bytes 98304 | tf_op jit(solution)/shard_map/all_gather | solution.py:125
  54.7 1.5 %shard_map.114 = f32[32,8,256]{2,1,0:T(8,128)S(1)} custom-call(s32[3,48]{1,0:T(4,128)S(1)} %add_add_fusion.index_ref, bf16[16,8,256]{2,1,0:T(8,128)(2,1)S(1)} %all_gather.20.source_ref, bf16[48,128,128]{2,1,0:T(8,128)(2,1)S(1)} %broadcast_select_fusion.tiles_ref), custom_call_target="tpu_custom_call" | custom-call | flops 12582912 | bytes 1572864 | tf_op jit(solution)/shard_map/pallas_call | solution.py:59
  56.2 16.3 %all_to_all.31 = f16[32,8,256]{2,1,0:T(8,128)(2,1)S(1)} all-to-all(f16[32,8,256]{2,1,0:T(8,128)(2,1)S(1)} %convert_element_type.100), channel_id=1, replica_groups=mesh['z'=8,'core'=2,'col'=32] {'col'}, dimensions={0} | all-to-all | bytes 262144 | tf_op jit(solution)/shard_map/all_to_all | solution.py:132
  72.6 13.0 %all_to_all.32.source_ref = bf16[32,8,256]{2,1,0:T(8,128)(2,1)S(1)} all-to-all(bf16[32,8,256]{2,1,0:T(8,128)(2,1)S(1)} %broadcast_in_dim.64), channel_id=1, replica_groups=mesh['z'=8,'core'=2,'col'=32] {'col'}, dimensions={0} | all-to-all | bytes 262144 | tf_op jit(solution)/shard_map/all_to_all | solution.py:27
  85.6 1.3 %shard_map.115 = f32[16,8,256]{2,1,0:T(8,128)S(1)} custom-call(s32[3,48]{1,0:T(4,128)S(1)} %add_add_fusion.index_ref, bf16[32,8,256]{2,1,0:T(8,128)(2,1)S(1)} %all_to_all.32.source_ref, bf16[48,128,128]{2,1,0:T(8,128)(2,1)S(1)} %broadcast_select_fusion.tiles_ref), custom_call_target="tpu_custom_call" | custom-call | flops 12582912 | bytes 1572864 | tf_op jit(solution)/shard_map/pallas_call | solution.py:59
  86.8 4.5 %all-gather.1 = f32[32,8,256]{2,1,0:T(8,128)S(1)} all-gather(f32[16,8,256]{2,1,0:T(8,128)S(1)} %shard_map.115), channel_id=3, replica_groups=mesh['z'=8,'core'=2,'col'=32] {'core'}, dimensions={0}, use_global_device_ids=true | all-gather | bytes 393216 | tf_op jit(solution)/shard_map/all_gather | solution.py:109
  91.4 14.8 %all_to_all.33 = f16[8,8,8,256]{3,2,1,0:T(8,128)(2,1)S(1)} all-to-all(f16[8,8,8,256]{3,2,1,0:T(8,128)(2,1)S(1)} %broadcast_in_dim.65), channel_id=1, replica_groups=mesh['z'=8,'core'=2,'col'=32] {'z'}, dimensions={0} | all-to-all | bytes 524288 | tf_op jit(solution)/shard_map/all_to_all | solution.py:27
  106.2 2.0 %all_gather.23.source_ref = bf16[16,8,256]{2,1,0:T(8,128)(2,1)S(1)} all-gather(bf16[8,8,256]{2,1,0:T(8,128)(2,1)S(1)} %get-tuple-element.20), channel_id=1, replica_groups=mesh['z'=8,'core'=2,'col'=32] {'core'}, dimensions={0}, use_global_device_ids=true | all-gather | bytes 98304 | tf_op jit(solution)/shard_map/all_gather | solution.py:125
  108.2 2.0 %shard_map.116 = (f32[32,8,256]{2,1,0:T(8,128)S(1)}, f32[8,256]{1,0:T(8,128)}) custom-call(s32[3,48]{1,0:T(4,128)S(1)} %add_add_fusion.index_ref, bf16[16,8,256]{2,1,0:T(8,128)(2,1)S(1)} %all_gather.23.source_ref, bf16[48,128,128]{2,1,0:T(8,128)(2,1)S(1)} %broadcast_select_fusion.tiles_ref, f32[8,8,256]{2,1,0:T(8,128)S(1)} %get-tuple-element.21.refs_0_), custom_call_target="tpu_custom_call" | custom-call | flops 12582912 | bytes 1572864 | tf_op jit(solution)/shard_map/pallas_call | solution.py:59
  110.2 12.3 %all_to_all.34 = f16[32,8,256]{2,1,0:T(8,128)(2,1)S(1)} all-to-all(f16[32,8,256]{2,1,0:T(8,128)(2,1)S(1)} %convert_element_type.106), channel_id=1, replica_groups=mesh['z'=8,'core'=2,'col'=32] {'col'}, dimensions={0} | all-to-all | bytes 262144 | tf_op jit(solution)/shard_map/all_to_all | solution.py:132
  (36 shorter events, 2.5 us)
Async XLA Ops:
  2.0 19.9 %all-to-all-start = ((bf16[32,8,256]{2,1,0:T(8,128)(2,1)}), bf16[32,8,256]{2,1,0:T(8,128)(2,1)S(1)}, u32[]{:S(2)}, u32[]{:S(2)}) async-start(bf16[32,8,256]{2,1,0:T(8,128)(2,1)} %broadcast_in_dim.30), calls=%async_computation | async-start | bytes 262144 | tf_op jit(solution)/shard_map/all_to_all | solution.py:27
  18.8 1.6 %copy-start.1 = (s32[48]{0:T(128)S(1)}, s32[48]{0:T(128)}, u32[]{:S(2)}) copy-start(s32[48]{0:T(128)} %param.17) | copy-start | bytes 580
  18.8 1.7 %copy-start = (f32[8,256]{1,0:T(8,128)S(1)}, f32[8,256]{1,0:T(8,128)}, u32[]{:S(2)}) copy-start(f32[8,256]{1,0:T(8,128)} %param.11) | copy-start | bytes 24580

commit v5 on v4

--- a/solution.py
+++ b/solution.py
@@ -15,7 +15,7 @@
 CORES = 2
 TILE_MAX, UPPER_MAX, DUAL_MAX, RHS_MAX = 0.125, 1.5, 1.0, 6.0
 HALF_MAX = 65504.0
-ROW_AT, COL_AT, PLANE = range(3)
+ROW_AT, COL_AT = range(2)
 
 
 def step_down(bound):
@@ -27,27 +27,40 @@
     return lax.all_to_all(copies, axis, 0, 0, tiled=True)
 
 
+def pack(parts):
+    size = sum(part.shape[0] for part in parts)
+    total, at = 0.0, 0
+    for part in parts:
+        rest = [(0, 0)] * (part.ndim - 1)
+        total = total + jnp.pad(part, [(at, size - at - part.shape[0]), *rest])
+        at += part.shape[0]
+    return lax.optimization_barrier(total)
+
+
 def tiles_kernel(contract, origins, targets, index_ref, source_ref, tiles_ref, *refs):
     state_ref, out_ref, own_ref, products_ref = refs if len(refs) == 4 else (None, refs[0], None, refs[1])
-    parts = out_ref.shape[-1] // LANES
-    source_parts = source_ref.shape[-1] // LANES
+    slots = tiles_ref.shape[0]
+    width, lanes = out_ref.shape[1], out_ref.shape[2]
     if state_ref is not None:
-        own_ref[...] = state_ref[index_ref[PLANE, 0]]
+        own_ref[...] = state_ref[lax.axis_index("z")]
+
+    def place(row, slot):
+        spot, parts = index_ref[row, slot], lanes // LANES
+        return spot // parts, slice(None), pl.ds(pl.multiple_of((spot % parts) * LANES, LANES), LANES)
+
+    def product(piece, tile):
+        return lax.dot_general(piece, tile, (((1,), (contract,)), ((), ())), preferred_element_type=jnp.float32)
+
     out_ref[...] = jnp.zeros_like(out_ref)
-    slots = tiles_ref.shape[0]
+    together = 2 if contract == 1 and slots % 2 == 0 else 1
+    for slot in range(0, slots, together):
+        pieces = [source_ref[place(origins, slot + i)] for i in range(together)]
+        tiles = [tiles_ref[slot + i] for i in range(together)]
+        found = product(jnp.concatenate(pieces, 0), jnp.concatenate(tiles, 0)) if together > 1 else product(pieces[0], tiles[0])
+        for i in range(together):
+            products_ref[slot + i] = found[i * width : (i + 1) * width, i * LANES : (i + 1) * LANES]
     for slot in range(slots):
-        origin = index_ref[origins, slot]
-        lanes = pl.ds(pl.multiple_of((origin % source_parts) * LANES, LANES), LANES)
-        products_ref[slot] = lax.dot_general(
-            source_ref[origin // source_parts, :, lanes],
-            tiles_ref[slot],
-            (((1,), (contract,)), ((), ())),
-            preferred_element_type=jnp.float32,
-        )
-    for slot in range(slots):
-        target = index_ref[targets, slot]
-        lanes = pl.ds(pl.multiple_of((target % parts) * LANES, LANES), LANES)
-        out_ref[target // parts, :, lanes] += products_ref[slot]
+        out_ref[place(targets, slot)] += products_ref[slot]
 
 
 def tile_products(contract, origins, targets, index, source, tiles, slabs, state=None):
@@ -84,17 +97,18 @@
     core = lax.axis_index("core")
     owner = tile_cols // per_piece
     tile_at = ((owner % CORES) * planes + owner // CORES) * per_piece + tile_cols % per_piece
-
-    index = jnp.stack([tile_rows, tile_at, jnp.full_like(tile_rows, lax.axis_index("z"))])
+    index = jnp.stack([tile_rows, tile_at])
     live = jnp.arange(slots, dtype=jnp.int32) < tile_count[0]
     tiles = jnp.where(live[:, None, None], tiles, jnp.zeros_like(tiles))
 
-    limits = jnp.pad(jnp.stack(split(upper)), ((0, width - 2), (0, 0)))
-    state = lax.optimization_barrier(jnp.stack([*split(primal), *split(cost), limits]))
-
-    pull = jnp.broadcast_to(DUAL_STEP * rhs[None, :], dual.shape)
-    floor = jnp.broadcast_to(jnp.where(row_kind == 1, 0.0, jnp.finfo(jnp.float32).min)[None, :], dual.shape)
-    lifted = lax.optimization_barrier(dual) + pull
+    floor = jnp.where(row_kind == 1, 0.0, jnp.finfo(jnp.float32).min)
+    x_own, cost_own, y = jnp.split(pack([primal, cost, lax.optimization_barrier(dual)]), 3)
+    vectors = jnp.split(pack([upper, rhs, floor]), 3)
+    upper_own, rhs_own, floor = (jnp.broadcast_to(vector[None], primal.shape) for vector in vectors)
+    first_row = lax.broadcasted_iota(jnp.int32, primal.shape, 0) == 0
+    state = jnp.stack([*split(x_own), *split(cost_own), jnp.where(first_row, *split(upper_own))])
+    pull = DUAL_STEP * rhs_own
+    lifted = y + pull
     y_sends = dual
     y_max = DUAL_MAX
     x_half = None

time: 124 us -> 120 us (0.968)
  blocking collectives: 94.3 us -> 91.4 us
  waiting for transfers between devices: 1.27 us -> 4.08 us
  other arithmetic: 8.93 us -> 6.21 us
    all_to_all x1, waiting for transfers between devices: 1.27 us -> 4.08 us  [to_all(): return lax.all_to_all(copies, axis, 0, 0, tiled=True)]
    all_to_all x2, blocking collectives: 28.6 us -> 25.8 us  [body(): lax.all_to_all((partial_image * scale).astype(jnp.float16), 'col', 0, 0,...]
    unnamed x4, other arithmetic: 2.84 us -> 0.06 us
    add x1 -> x3, other arithmetic: 0.01 us -> 1.44 us  [the longest x2 1.43 us: pack(): total = total + jnp.pad(part, [(at, size - at - part.shape[0]), *rest])]
  transfers between devices with their start and end apart: 1 -> 1, of which waited for: 1 -> 1; matrix products, arithmetic and copies ran while one was open for 6% -> 4% of each run, Pallas kernels for 0% -> 0%
where the time goes in v5:
time: 120 us
  blocking collectives  91.4 us (76%)
  starting transfers between devices  10.5 us (9%)
  other arithmetic  6.21 us (5%)
  Pallas kernels  5.51 us (5%)
  waiting for transfers between devices  4.08 us (3%)
  between operations  1.43 us (1%)
    all_to_all x3, blocking collectives, to_all(): return lax.all_to_all(copies, axis, 0, 0, tiled=True)  52.2 us
    all_to_all x2, blocking collectives, body(): lax.all_to_all((partial_image * scale).astype(jnp.float16), 'col', 0, 0,...  25.8 us
    all_to_all x1, starting transfers between devices, to_all(): return lax.all_to_all(copies, axis, 0, 0, tiled=True)  10.5 us
    all_gather x2, blocking collectives, body(): lax.all_gather(partial_grad, 'core', axis=0)  8.19 us
    pallas_call x4, Pallas kernels, tile_products(): pl.pallas_call(functools.partial(tiles_kernel, contract, origins, targets...  5.51 us
    all_gather x2, blocking collectives, body(): x_cols = lax.all_gather(xbar, 'core', axis=0, tiled=True)  5.23 us
    all_to_all x1, waiting for transfers between devices, to_all(): return lax.all_to_all(copies, axis, 0, 0, tiled=True)  4.08 us
  transfers between devices with their start and end apart: 1, of which 1 were waited for; matrix products, arithmetic and copies ran while one was open for 4% of the time, Pallas kernels for 0%

profile of v5, /device:TPU:1, one launch (start us, length us, event | category | flops | bytes accessed | tf_op | source)
XLA Modules:
  0.0 119.9 jit_solution(4979527859865138666)
XLA Ops:
  0.6 0.7 convert_element_type.97
  1.3 0.6 broadcast_in_dim.34
  2.0 10.5 %all-to-all-start = ((bf16[32,8,256]{2,1,0:T(8,128)(2,1)}), bf16[32,8,256]{2,1,0:T(8,128)(2,1)S(1)}, u32[]{:S(2)}, u32[]{:S(2)}) async-start(bf16[32,8,256]{2,1,0:T(8,128)(2,1)} %broadcast_in_dim.34), calls=%async_computation | async-start | bytes 262144 | tf_op jit(solution)/shard_map/all_to_all | solution.py:27
  13.2 0.7 fusion.21
  13.8 0.7 compare_select_fusion
  14.5 0.7 pad_add_fusion.1
  15.2 0.7 pad_add_fusion
  16.1 1.6 %broadcast_select_fusion.tiles_ref = bf16[48,128,128]{2,1,0:T(8,128)(2,1)S(1)} fusion(bf16[48,128,128]{2,1,0:T(8,128)(2,1)} %param.16, pred[48]{0:T(512)(128)(4,1)S(1)} %iota_compare_fusion.1), kind=kLoop, calls=%fused_computation | loop fusion | flops 786432 | bytes 3145776 | tf_op jit(solution)/shard_map/jit(_where)/select_n | solution.py:102
  17.6 0.1 constant_dynamic-update-slice_fusion
  17.8 4.1 %all-to-all-done.source_ref = bf16[32,8,256]{2,1,0:T(8,128)(2,1)S(1)} async-done(((bf16[32,8,256]{2,1,0:T(8,128)(2,1)}), bf16[32,8,256]{2,1,0:T(8,128)(2,1)S(1)}, u32[]{:S(2)}, u32[]{:S(2)}) %all-to-all-start) | async-done | bytes 131104 | tf_op jit(solution)/shard_map/all_to_all | solution.py:27
  21.8 1.2 %shard_map.113 = f32[16,8,256]{2,1,0:T(8,128)S(1)} custom-call(s32[2,48]{1,0:T(2,128)S(1)} %pad_add_fusion.2.index_ref, bf16[32,8,256]{2,1,0:T(8,128)(2,1)S(1)} %all-to-all-done.source_ref, bf16[48,128,128]{2,1,0:T(8,128)(2,1)S(1)} %broadcast_select_fusion.tiles_ref), custom_call_target="tpu_custom_call" | custom-call | flops 12582912 | bytes 1572864 | tf_op jit(solution)/shard_map/pallas_call | solution.py:72
  23.1 3.7 %all-gather = f32[32,8,256]{2,1,0:T(8,128)S(1)} all-gather(f32[16,8,256]{2,1,0:T(8,128)S(1)} %shard_map.113), channel_id=2, replica_groups=mesh['z'=8,'core'=2,'col'=32] {'core'}, dimensions={0}, use_global_device_ids=true | all-gather | bytes 393216 | tf_op jit(solution)/shard_map/all_gather | solution.py:123
  26.8 24.4 %all_to_all.30 = f16[8,13,8,256]{3,2,1,0:T(8,128)(2,1)S(1)} all-to-all(f16[8,13,8,256]{3,2,1,0:T(8,128)(2,1)S(1)} %broadcast_in_dim.73), channel_id=1, replica_groups=mesh['z'=8,'core'=2,'col'=32] {'z'}, dimensions={0} | all-to-all | bytes 851968 | tf_op jit(solution)/shard_map/all_to_all | solution.py:27
  51.4 3.2 %all_gather.20.source_ref = bf16[16,8,256]{2,1,0:T(8,128)(2,1)S(1)} all-gather(bf16[8,8,256]{2,1,0:T(8,128)(2,1)S(1)} %get-tuple-element.22), channel_id=1, replica_groups=mesh['z'=8,'core'=2,'col'=32] {'core'}, dimensions={0}, use_global_device_ids=true | all-gather | bytes 98304 | tf_op jit(solution)/shard_map/all_gather | solution.py:139
  54.7 1.2 %shard_map.114 = f32[32,8,256]{2,1,0:T(8,128)S(1)} custom-call(s32[2,48]{1,0:T(2,128)S(1)} %pad_add_fusion.2.index_ref, bf16[16,8,256]{2,1,0:T(8,128)(2,1)S(1)} %all_gather.20.source_ref, bf16[48,128,128]{2,1,0:T(8,128)(2,1)S(1)} %broadcast_select_fusion.tiles_ref), custom_call_target="tpu_custom_call" | custom-call | flops 12582912 | bytes 1572864 | tf_op jit(solution)/shard_map/pallas_call | solution.py:72
  55.9 13.5 %all_to_all.31 = f16[32,8,256]{2,1,0:T(8,128)(2,1)S(1)} all-to-all(f16[32,8,256]{2,1,0:T(8,128)(2,1)S(1)} %convert_element_type.113), channel_id=1, replica_groups=mesh['z'=8,'core'=2,'col'=32] {'col'}, dimensions={0} | all-to-all | bytes 262144 | tf_op jit(solution)/shard_map/all_to_all | solution.py:146
  69.5 13.0 %all_to_all.32.source_ref = bf16[32,8,256]{2,1,0:T(8,128)(2,1)S(1)} all-to-all(bf16[32,8,256]{2,1,0:T(8,128)(2,1)S(1)} %broadcast_in_dim.74), channel_id=1, replica_groups=mesh['z'=8,'core'=2,'col'=32] {'col'}, dimensions={0} | all-to-all | bytes 262144 | tf_op jit(solution)/shard_map/all_to_all | solution.py:27
  82.5 1.2 %shard_map.115 = f32[16,8,256]{2,1,0:T(8,128)S(1)} custom-call(s32[2,48]{1,0:T(2,128)S(1)} %pad_add_fusion.2.index_ref, bf16[32,8,256]{2,1,0:T(8,128)(2,1)S(1)} %all_to_all.32.source_ref, bf16[48,128,128]{2,1,0:T(8,128)(2,1)S(1)} %broadcast_select_fusion.tiles_ref), custom_call_target="tpu_custom_call" | custom-call | flops 12582912 | bytes 1572864 | tf_op jit(solution)/shard_map/pallas_call | solution.py:72
  83.7 4.5 %all-gather.1 = f32[32,8,256]{2,1,0:T(8,128)S(1)} all-gather(f32[16,8,256]{2,1,0:T(8,128)S(1)} %shard_map.115), channel_id=3, replica_groups=mesh['z'=8,'core'=2,'col'=32] {'core'}, dimensions={0}, use_global_device_ids=true | all-gather | bytes 393216 | tf_op jit(solution)/shard_map/all_gather | solution.py:123
  88.3 14.8 %all_to_all.33 = f16[8,8,8,256]{3,2,1,0:T(8,128)(2,1)S(1)} all-to-all(f16[8,8,8,256]{3,2,1,0:T(8,128)(2,1)S(1)} %broadcast_in_dim.75), channel_id=1, replica_groups=mesh['z'=8,'core'=2,'col'=32] {'z'}, dimensions={0} | all-to-all | bytes 524288 | tf_op jit(solution)/shard_map/all_to_all | solution.py:27
  103.1 2.0 %all_gather.23.source_ref = bf16[16,8,256]{2,1,0:T(8,128)(2,1)S(1)} all-gather(bf16[8,8,256]{2,1,0:T(8,128)(2,1)S(1)} %get-tuple-element.20), channel_id=1, replica_groups=mesh['z'=8,'core'=2,'col'=32] {'core'}, dimensions={0}, use_global_device_ids=true | all-gather | bytes 98304 | tf_op jit(solution)/shard_map/all_gather | solution.py:139
  105.1 1.8 %shard_map.116 = (f32[32,8,256]{2,1,0:T(8,128)S(1)}, f32[8,256]{1,0:T(8,128)}) custom-call(s32[2,48]{1,0:T(2,128)S(1)} %pad_add_fusion.2.index_ref, bf16[16,8,256]{2,1,0:T(8,128)(2,1)S(1)} %all_gather.23.source_ref, bf16[48,128,128]{2,1,0:T(8,128)(2,1)S(1)} %broadcast_select_fusion.tiles_ref, f32[8,8,256]{2,1,0:T(8,128)S(1)} %get-tuple-element.21.refs_0_), custom_call_target="tpu_custom_call" | custom-call | flops 12582912 | bytes 1572864 | tf_op jit(solution)/shard_map/pallas_call | solution.py:72
  107.0 12.3 %all_to_all.34 = f16[32,8,256]{2,1,0:T(8,128)(2,1)S(1)} all-to-all(f16[32,8,256]{2,1,0:T(8,128)(2,1)S(1)} %convert_element_type.119), channel_id=1, replica_groups=mesh['z'=8,'core'=2,'col'=32] {'col'}, dimensions={0} | all-to-all | bytes 262144 | tf_op jit(solution)/shard_map/all_to_all | solution.py:146
  119.3 0.6 subtract_maximum_fusion
  (33 shorter events, 0.5 us)
Async XLA Ops:
  2.0 19.9 %all-to-all-start = ((bf16[32,8,256]{2,1,0:T(8,128)(2,1)}), bf16[32,8,256]{2,1,0:T(8,128)(2,1)S(1)}, u32[]{:S(2)}, u32[]{:S(2)}) async-start(bf16[32,8,256]{2,1,0:T(8,128)(2,1)} %broadcast_in_dim.34), calls=%async_computation | async-start | bytes 262144 | tf_op jit(solution)/shard_map/all_to_all | solution.py:27
  16.0 1.7 %copy-start = (s32[48]{0:T(128)S(1)}, s32[48]{0:T(128)}, u32[]{:S(2)}) copy-start(s32[48]{0:T(128)} %param.17) | copy-start | bytes 580

commit v6 on v5

--- a/solution.py
+++ b/solution.py
@@ -22,14 +22,15 @@
     return 2.0 ** min(0, math.floor(math.log2(0.95 * HALF_MAX / bound)))
 
 
-def to_all(piece, axis, dtype):
-    copies = jnp.broadcast_to(piece[None], (lax.axis_size(axis), *piece.shape)).astype(dtype)
+def to_all(piece, axis, dtype, fresh=False):
+    zeros = lax.optimization_barrier(jnp.zeros((lax.axis_size(axis), 1, 1), piece.dtype)) if fresh else 0.0
+    copies = jnp.broadcast_to(piece[None] + zeros, (lax.axis_size(axis), *piece.shape)).astype(dtype)
     return lax.all_to_all(copies, axis, 0, 0, tiled=True)
 
 
 def pack(parts):
     size = sum(part.shape[0] for part in parts)
-    total, at = 0.0, 0
+    total, at = 0, 0
     for part in parts:
         rest = [(0, 0)] * (part.ndim - 1)
         total = total + jnp.pad(part, [(at, size - at - part.shape[0]), *rest])
@@ -37,12 +38,9 @@
     return lax.optimization_barrier(total)
 
 
-def tiles_kernel(contract, origins, targets, index_ref, source_ref, tiles_ref, *refs):
-    state_ref, out_ref, own_ref, products_ref = refs if len(refs) == 4 else (None, refs[0], None, refs[1])
+def tiles_kernel(contract, origins, targets, index_ref, source_ref, tiles_ref, out_ref, products_ref):
     slots = tiles_ref.shape[0]
     width, lanes = out_ref.shape[1], out_ref.shape[2]
-    if state_ref is not None:
-        own_ref[...] = state_ref[lax.axis_index("z")]
 
     def place(row, slot):
         spot, parts = index_ref[row, slot], lanes // LANES
@@ -63,23 +61,41 @@
         out_ref[place(targets, slot)] += products_ref[slot]
 
 
-def tile_products(contract, origins, targets, index, source, tiles, slabs, state=None):
+def tile_products(contract, origins, targets, index, source, tiles, slabs):
     smem, vmem = pl.BlockSpec(memory_space=pltpu.SMEM), pl.BlockSpec(memory_space=pltpu.VMEM)
     slots, width, lanes = tiles.shape[0], source.shape[1], source.shape[2]
-    out = jax.ShapeDtypeStruct((slabs, width, lanes), jnp.float32)
-    own = jax.ShapeDtypeStruct((width, lanes), jnp.float32)
-    extra = () if state is None else (state,)
     return pl.pallas_call(
         functools.partial(tiles_kernel, contract, origins, targets),
-        out_shape=out if state is None else (out, own),
-        in_specs=[smem, vmem, vmem] + [vmem] * len(extra),
-        out_specs=vmem if state is None else (vmem, vmem),
+        out_shape=jax.ShapeDtypeStruct((slabs, width, lanes), jnp.float32),
+        in_specs=[smem, vmem, vmem],
+        out_specs=vmem,
         scratch_shapes=[pltpu.VMEM((slots, width, LANES), jnp.float32)],
         cost_estimate=pl.CostEstimate(
             flops=2 * slots * width * LANES * LANES, bytes_accessed=tiles.size * 2, transcendentals=0
         ),
         compiler_params=pltpu.CompilerParams(vmem_limit_bytes=16 * 2**20),
-    )(index, source, tiles, *extra)
+    )(index, source, tiles)
+
+
+def results_kernel(steps, lifted_ref, pull_ref, floor_ref, x_ref, *refs):
+    *image_refs, primal_ref, dual_ref = refs
+    primal_ref[...] = x_ref[lax.axis_index("z")]
+    lifted = lifted_ref[...]
+    for step, image_ref in zip(steps, image_refs):
+        y = jnp.maximum(lifted - step * image_ref[...], floor_ref[...])
+        lifted = y + pull_ref[...]
+    dual_ref[...] = y
+
+
+def results(steps, lifted, pull, floor, x_half, images):
+    vmem = pl.BlockSpec(memory_space=pltpu.VMEM)
+    return pl.pallas_call(
+        functools.partial(results_kernel, steps),
+        out_shape=(jax.ShapeDtypeStruct(lifted.shape, jnp.float32),) * 2,
+        in_specs=[vmem] * (4 + len(images)),
+        out_specs=(vmem, vmem),
+        compiler_params=pltpu.CompilerParams(vmem_limit_bytes=16 * 2**20),
+    )(lifted, pull, floor, x_half, *images)
 
 
 def split(value):
@@ -95,16 +111,18 @@
     col_tiles = per_piece * planes * CORES
     row_tiles = per_piece * col_devices
     core = lax.axis_index("core")
-    owner = tile_cols // per_piece
-    tile_at = ((owner % CORES) * planes + owner // CORES) * per_piece + tile_cols % per_piece
-    index = jnp.stack([tile_rows, tile_at])
     live = jnp.arange(slots, dtype=jnp.int32) < tile_count[0]
     tiles = jnp.where(live[:, None, None], tiles, jnp.zeros_like(tiles))
 
-    floor = jnp.where(row_kind == 1, 0.0, jnp.finfo(jnp.float32).min)
     x_own, cost_own, y = jnp.split(pack([primal, cost, lax.optimization_barrier(dual)]), 3)
-    vectors = jnp.split(pack([upper, rhs, floor]), 3)
-    upper_own, rhs_own, floor = (jnp.broadcast_to(vector[None], primal.shape) for vector in vectors)
+    upper_own, rhs_own = jnp.split(pack([upper, rhs]), 2)
+    kind, rows, cols = jnp.split(pack([row_kind, tile_rows, tile_cols]), [piece, piece + slots])
+    floor = jnp.where(kind == 1, 0.0, jnp.finfo(jnp.float32).min)
+    upper_own, rhs_own, floor = (jnp.broadcast_to(vector[None], primal.shape) for vector in (upper_own, rhs_own, floor))
+    owner = cols // per_piece
+    tile_at = ((owner % CORES) * planes + owner // CORES) * per_piece + cols % per_piece
+    index = jnp.stack([rows, tile_at])
+
     first_row = lax.broadcasted_iota(jnp.int32, primal.shape, 0) == 0
     state = jnp.stack([*split(x_own), *split(cost_own), jnp.where(first_row, *split(upper_own))])
     pull = DUAL_STEP * rhs_own
@@ -113,11 +131,12 @@
     y_max = DUAL_MAX
     x_half = None
     for step in range(ITERS):
-        y_rows = to_all(y_sends, "col", jnp.bfloat16)
+        y_rows = to_all(y_sends, "col", jnp.bfloat16, fresh=step == 0)
         if step == 0:
             y_rows, index, tiles, state, lifted, pull, floor = lax.optimization_barrier(
                 (y_rows, index, tiles, state, lifted, pull, floor)
             )
+            raised, images, steps = lifted, [], []
         partial_grad = tile_products(0, ROW_AT, COL_AT, index, y_rows, tiles, CORES * planes)
 
         both = lax.all_gather(partial_grad, "core", axis=0).reshape(CORES, CORES, planes, width, piece)
@@ -137,18 +156,17 @@
         x_new = jnp.clip(x_half - PRIMAL_STEP * (cost_half - grad), 0.0, upper_half)
         xbar = (2.0 * x_new - x_half).astype(jnp.bfloat16)
         x_cols = lax.all_gather(xbar, "core", axis=0, tiled=True)
-        last = step == ITERS - 1
-        partial_image = tile_products(1, COL_AT, ROW_AT, index, x_cols, tiles, col_devices, x_new if last else None)
-        if last:
-            partial_image, primal_out = partial_image
+        partial_image = tile_products(1, COL_AT, ROW_AT, index, x_cols, tiles, col_devices)
         h_max = min(slots, col_tiles) * LANES * TILE_MAX * 2 * UPPER_MAX
         scale = step_down(h_max)
         got = lax.all_to_all((partial_image * scale).astype(jnp.float16), "col", 0, 0, tiled=True)
         image = jnp.sum(got.astype(jnp.float32), axis=0)
-        y = jnp.maximum(lifted - (DUAL_STEP / scale) * image, floor)
+        images.append(image)
+        steps.append(DUAL_STEP / scale)
+        y = jnp.maximum(raised - steps[-1] * image, floor)
         y_max = y_max + DUAL_STEP * (RHS_MAX + col_devices * h_max)
-        y_sends, lifted, x_half = y, y + pull, x_new
-    return primal_out, y
+        y_sends, raised, x_half = y, y + pull, x_new
+    return results(tuple(steps), lifted, pull, floor, x_half, images)
 
 
 def solution(mesh):

time: 120 us -> 120 us (level)
  transfers between devices with their start and end apart: 1 -> 1, of which waited for: 1 -> 1; matrix products, arithmetic and copies ran while one was open for 4% -> 3% of each run, Pallas kernels for 0% -> 0%
where the time goes in v6:
time: 120 us; the launch traced here: 119 us
  blocking collectives  91 us (76%)
  starting transfers between devices  10.5 us (9%)
  other arithmetic  5.86 us (5%)
  Pallas kernels  5.53 us (5%)
  waiting for transfers between devices  4.57 us (4%)
  between operations  1.45 us (1%)
    all_to_all x3, blocking collectives, to_all(): return lax.all_to_all(copies, axis, 0, 0, tiled=True)  52.2 us
    all_to_all x2, blocking collectives, body(): lax.all_to_all((partial_image * scale).astype(jnp.float16), 'col', 0, 0,...  25.3 us
    all_to_all x1, starting transfers between devices, to_all(): return lax.all_to_all(copies, axis, 0, 0, tiled=True)  10.5 us
    all_gather x2, blocking collectives, body(): lax.all_gather(partial_grad, 'core', axis=0)  8.19 us
    all_gather x2, blocking collectives, body(): x_cols = lax.all_gather(xbar, 'core', axis=0, tiled=True)  5.23 us
    pallas_call x4, Pallas kernels, tile_products(): pl.pallas_call(functools.partial(tiles_kernel, contract, origins, targets...  4.91 us
    all_to_all x1, waiting for transfers between devices, to_all(): return lax.all_to_all(copies, axis, 0, 0, tiled=True)  4.57 us
  transfers between devices with their start and end apart: 1, of which 1 were waited for; matrix products, arithmetic and copies ran while one was open for 3% of the time, Pallas kernels for 0%

profile of v6, /device:TPU:1, one launch (start us, length us, event | category | flops | bytes accessed | tf_op | source)
XLA Modules:
  0.0 118.9 jit_solution(2564389570972354551)
XLA Ops:
  0.6 1.4 %add_convert_fusion = bf16[32,8,256]{2,1,0:T(8,128)(2,1)} fusion(f32[32]{0:T(128)S(1)} %bitcast.94, f32[8,256]{1,0:T(8,128)} %param.11), kind=kLoop, calls=%fused_computation.5 | loop fusion | flops 131072 | bytes 139392 | tf_op jit(solution)/shard_map/convert_element_type | solution.py:27
  2.1 10.5 %all-to-all-start = ((bf16[32,8,256]{2,1,0:T(8,128)(2,1)}), bf16[32,8,256]{2,1,0:T(8,128)(2,1)S(1)}, u32[]{:S(2)}, u32[]{:S(2)}) async-start(bf16[32,8,256]{2,1,0:T(8,128)(2,1)} %add_convert_fusion), calls=%async_computation | async-start | bytes 262144 | tf_op jit(solution)/shard_map/all_to_all | solution.py:28
  12.6 0.8 pad_add_fusion.2
  13.4 0.1 slice_bitcast_fusion.5
  14.2 0.7 pad_add_fusion.1
  14.9 0.7 pad_add_fusion
  15.7 1.6 %broadcast_select_fusion.tiles_ref = bf16[48,128,128]{2,1,0:T(8,128)(2,1)S(1)} fusion(bf16[48,128,128]{2,1,0:T(8,128)(2,1)} %param.16, pred[48]{0:T(512)(128)(4,1)S(1)} %iota_compare_fusion.1), kind=kLoop, calls=%fused_computation | loop fusion | flops 786432 | bytes 3145776 | tf_op jit(solution)/shard_map/jit(_where)/select_n | solution.py:115
  17.3 0.1 constant_dynamic-update-slice_fusion
  17.4 4.6 %all-to-all-done.source_ref = bf16[32,8,256]{2,1,0:T(8,128)(2,1)S(1)} async-done(((bf16[32,8,256]{2,1,0:T(8,128)(2,1)}), bf16[32,8,256]{2,1,0:T(8,128)(2,1)S(1)}, u32[]{:S(2)}, u32[]{:S(2)}) %all-to-all-start) | async-done | bytes 131104 | tf_op jit(solution)/shard_map/all_to_all | solution.py:28
  21.9 1.2 %shard_map.113 = f32[16,8,256]{2,1,0:T(8,128)S(1)} custom-call(s32[2,48]{1,0:T(2,128)S(1)} %pad_add_fusion.3.index_ref, bf16[32,8,256]{2,1,0:T(8,128)(2,1)S(1)} %all-to-all-done.source_ref, bf16[48,128,128]{2,1,0:T(8,128)(2,1)S(1)} %broadcast_select_fusion.tiles_ref), custom_call_target="tpu_custom_call" | custom-call | flops 12582912 | bytes 1572864 | tf_op jit(solution)/shard_map/pallas_call | solution.py:67
  23.2 3.7 %all-gather = f32[32,8,256]{2,1,0:T(8,128)S(1)} all-gather(f32[16,8,256]{2,1,0:T(8,128)S(1)} %shard_map.113), channel_id=2, replica_groups=mesh['z'=8,'core'=2,'col'=32] {'core'}, dimensions={0}, use_global_device_ids=true | all-gather | bytes 393216 | tf_op jit(solution)/shard_map/all_gather | solution.py:142
  26.9 24.4 %all_to_all.30 = f16[8,13,8,256]{3,2,1,0:T(8,128)(2,1)S(1)} all-to-all(f16[8,13,8,256]{3,2,1,0:T(8,128)(2,1)S(1)} %broadcast_in_dim.71), channel_id=1, replica_groups=mesh['z'=8,'core'=2,'col'=32] {'z'}, dimensions={0} | all-to-all | bytes 851968 | tf_op jit(solution)/shard_map/all_to_all | solution.py:28
  51.5 3.2 %all_gather.20.source_ref = bf16[16,8,256]{2,1,0:T(8,128)(2,1)S(1)} all-gather(bf16[8,8,256]{2,1,0:T(8,128)(2,1)S(1)} %get-tuple-element.18), channel_id=1, replica_groups=mesh['z'=8,'core'=2,'col'=32] {'core'}, dimensions={0}, use_global_device_ids=true | all-gather | bytes 98304 | tf_op jit(solution)/shard_map/all_gather | solution.py:158
  54.8 1.2 %shard_map.114 = f32[32,8,256]{2,1,0:T(8,128)S(1)} custom-call(s32[2,48]{1,0:T(2,128)S(1)} %pad_add_fusion.3.index_ref, bf16[16,8,256]{2,1,0:T(8,128)(2,1)S(1)} %all_gather.20.source_ref, bf16[48,128,128]{2,1,0:T(8,128)(2,1)S(1)} %broadcast_select_fusion.tiles_ref), custom_call_target="tpu_custom_call" | custom-call | flops 12582912 | bytes 1572864 | tf_op jit(solution)/shard_map/pallas_call | solution.py:67
  56.0 13.0 %all_to_all.31 = f16[32,8,256]{2,1,0:T(8,128)(2,1)S(1)} all-to-all(f16[32,8,256]{2,1,0:T(8,128)(2,1)S(1)} %convert_element_type.110), channel_id=1, replica_groups=mesh['z'=8,'core'=2,'col'=32] {'col'}, dimensions={0} | all-to-all | bytes 262144 | tf_op jit(solution)/shard_map/all_to_all | solution.py:162
  69.1 13.0 %all_to_all.32.source_ref = bf16[32,8,256]{2,1,0:T(8,128)(2,1)S(1)} all-to-all(bf16[32,8,256]{2,1,0:T(8,128)(2,1)S(1)} %broadcast_in_dim.72), channel_id=1, replica_groups=mesh['z'=8,'core'=2,'col'=32] {'col'}, dimensions={0} | all-to-all | bytes 262144 | tf_op jit(solution)/shard_map/all_to_all | solution.py:28
  82.1 1.2 %shard_map.115 = f32[16,8,256]{2,1,0:T(8,128)S(1)} custom-call(s32[2,48]{1,0:T(2,128)S(1)} %pad_add_fusion.3.index_ref, bf16[32,8,256]{2,1,0:T(8,128)(2,1)S(1)} %all_to_all.32.source_ref, bf16[48,128,128]{2,1,0:T(8,128)(2,1)S(1)} %broadcast_select_fusion.tiles_ref), custom_call_target="tpu_custom_call" | custom-call | flops 12582912 | bytes 1572864 | tf_op jit(solution)/shard_map/pallas_call | solution.py:67
  83.3 4.5 %all-gather.1 = f32[32,8,256]{2,1,0:T(8,128)S(1)} all-gather(f32[16,8,256]{2,1,0:T(8,128)S(1)} %shard_map.115), channel_id=3, replica_groups=mesh['z'=8,'core'=2,'col'=32] {'core'}, dimensions={0}, use_global_device_ids=true | all-gather | bytes 393216 | tf_op jit(solution)/shard_map/all_gather | solution.py:142
  87.9 14.8 %all_to_all.33 = f16[8,8,8,256]{3,2,1,0:T(8,128)(2,1)S(1)} all-to-all(f16[8,8,8,256]{3,2,1,0:T(8,128)(2,1)S(1)} %broadcast_in_dim.73), channel_id=1, replica_groups=mesh['z'=8,'core'=2,'col'=32] {'z'}, dimensions={0} | all-to-all | bytes 524288 | tf_op jit(solution)/shard_map/all_to_all | solution.py:28
  102.7 2.0 %all_gather.23.source_ref = bf16[16,8,256]{2,1,0:T(8,128)(2,1)S(1)} all-gather(bf16[8,8,256]{2,1,0:T(8,128)(2,1)S(1)} %get-tuple-element.16), channel_id=1, replica_groups=mesh['z'=8,'core'=2,'col'=32] {'core'}, dimensions={0}, use_global_device_ids=true | all-gather | bytes 98304 | tf_op jit(solution)/shard_map/all_gather | solution.py:158
  104.7 1.2 %shard_map.116 = f32[32,8,256]{2,1,0:T(8,128)S(1)} custom-call(s32[2,48]{1,0:T(2,128)S(1)} %pad_add_fusion.3.index_ref, bf16[16,8,256]{2,1,0:T(8,128)(2,1)S(1)} %all_gather.23.source_ref, bf16[48,128,128]{2,1,0:T(8,128)(2,1)S(1)} %broadcast_select_fusion.tiles_ref), custom_call_target="tpu_custom_call" | custom-call | flops 12582912 | bytes 1572864 | tf_op jit(solution)/shard_map/pallas_call | solution.py:67
  106.0 12.3 %all_to_all.34 = f16[32,8,256]{2,1,0:T(8,128)(2,1)S(1)} all-to-all(f16[32,8,256]{2,1,0:T(8,128)(2,1)S(1)} %convert_element_type.116), channel_id=1, replica_groups=mesh['z'=8,'core'=2,'col'=32] {'col'}, dimensions={0} | all-to-all | bytes 262144 | tf_op jit(solution)/shard_map/all_to_all | solution.py:162
  118.3 0.6 shard_map.117
  (33 shorter events, 0.5 us)
Async XLA Ops:
  2.1 19.9 %all-to-all-start = ((bf16[32,8,256]{2,1,0:T(8,128)(2,1)}), bf16[32,8,256]{2,1,0:T(8,128)(2,1)S(1)}, u32[]{:S(2)}, u32[]{:S(2)}) async-start(bf16[32,8,256]{2,1,0:T(8,128)(2,1)} %add_convert_fusion), calls=%async_computation | async-start | bytes 262144 | tf_op jit(solution)/shard_map/all_to_all | solution.py:28

commit v7 on v6

--- a/solution.py
+++ b/solution.py
@@ -114,11 +114,11 @@
     live = jnp.arange(slots, dtype=jnp.int32) < tile_count[0]
     tiles = jnp.where(live[:, None, None], tiles, jnp.zeros_like(tiles))
 
-    x_own, cost_own, y = jnp.split(pack([primal, cost, lax.optimization_barrier(dual)]), 3)
-    upper_own, rhs_own = jnp.split(pack([upper, rhs]), 2)
+    fields = pack([primal, cost, lax.optimization_barrier(dual), upper[None], rhs[None]])
+    x_own, cost_own, y, upper_own, rhs_own = jnp.split(fields, [width, 2 * width, 3 * width, 3 * width + 1])
     kind, rows, cols = jnp.split(pack([row_kind, tile_rows, tile_cols]), [piece, piece + slots])
     floor = jnp.where(kind == 1, 0.0, jnp.finfo(jnp.float32).min)
-    upper_own, rhs_own, floor = (jnp.broadcast_to(vector[None], primal.shape) for vector in (upper_own, rhs_own, floor))
+    upper_own, rhs_own, floor = (jnp.broadcast_to(row, primal.shape) for row in (upper_own, rhs_own, floor[None]))
     owner = cols // per_piece
     tile_at = ((owner % CORES) * planes + owner // CORES) * per_piece + cols % per_piece
     index = jnp.stack([rows, tile_at])

time: 120 us -> 119 us (level)
  no operation moved by 1% of the time
where the time goes in v7:
time: 119 us; the launch traced here: 118 us
  blocking collectives  90.4 us (76%)
  starting transfers between devices  10.5 us (9%)
  Pallas kernels  5.53 us (5%)
  waiting for transfers between devices  5.22 us (4%)
  other arithmetic  5.2 us (4%)
  between operations  1.45 us (1%)
    all_to_all x3, blocking collectives, to_all(): return lax.all_to_all(copies, axis, 0, 0, tiled=True)  52.2 us
    all_to_all x2, blocking collectives, body(): lax.all_to_all((partial_image * scale).astype(jnp.float16), 'col', 0, 0,...  24.7 us
    all_to_all x1, starting transfers between devices, to_all(): return lax.all_to_all(copies, axis, 0, 0, tiled=True)  10.5 us
    all_gather x2, blocking collectives, body(): lax.all_gather(partial_grad, 'core', axis=0)  8.19 us
    all_gather x2, blocking collectives, body(): x_cols = lax.all_gather(xbar, 'core', axis=0, tiled=True)  5.23 us
    all_to_all x1, waiting for transfers between devices, to_all(): return lax.all_to_all(copies, axis, 0, 0, tiled=True)  5.22 us
    pallas_call x4, Pallas kernels, tile_products(): pl.pallas_call(functools.partial(tiles_kernel, contract, origins, targets...  4.91 us
  transfers between devices with their start and end apart: 1, of which 1 were waited for; matrix products, arithmetic and copies ran while one was open for 3% of the time, Pallas kernels for 0%

profile of v7, /device:TPU:1, one launch (start us, length us, event | category | flops | bytes accessed | tf_op | source)
XLA Modules:
  0.0 118.3 jit_solution(16418522700697479191)
XLA Ops:
  0.6 1.4 %add_convert_fusion = bf16[32,8,256]{2,1,0:T(8,128)(2,1)} fusion(f32[32]{0:T(128)S(1)} %bitcast.103, f32[8,256]{1,0:T(8,128)} %param.11), kind=kLoop, calls=%fused_computation.5 | loop fusion | flops 131072 | bytes 139392 | tf_op jit(solution)/shard_map/convert_element_type | solution.py:27
  2.1 10.5 %all-to-all-start = ((bf16[32,8,256]{2,1,0:T(8,128)(2,1)}), bf16[32,8,256]{2,1,0:T(8,128)(2,1)S(1)}, u32[]{:S(2)}, u32[]{:S(2)}) async-start(bf16[32,8,256]{2,1,0:T(8,128)(2,1)} %add_convert_fusion), calls=%async_computation | async-start | bytes 262144 | tf_op jit(solution)/shard_map/all_to_all | solution.py:28
  12.6 0.8 pad_add_fusion.1
  13.4 0.1 slice_bitcast_fusion.5
  13.5 0.8 pad_add_fusion
  15.0 1.6 %broadcast_select_fusion.tiles_ref = bf16[48,128,128]{2,1,0:T(8,128)(2,1)S(1)} fusion(bf16[48,128,128]{2,1,0:T(8,128)(2,1)} %param.16, pred[48]{0:T(512)(128)(4,1)S(1)} %iota_compare_fusion.1), kind=kLoop, calls=%fused_computation | loop fusion | flops 786432 | bytes 3145776 | tf_op jit(solution)/shard_map/jit(_where)/select_n | solution.py:115
  16.6 0.1 constant_dynamic-update-slice_fusion
  16.7 5.2 %all-to-all-done.source_ref = bf16[32,8,256]{2,1,0:T(8,128)(2,1)S(1)} async-done(((bf16[32,8,256]{2,1,0:T(8,128)(2,1)}), bf16[32,8,256]{2,1,0:T(8,128)(2,1)S(1)}, u32[]{:S(2)}, u32[]{:S(2)}) %all-to-all-start) | async-done | bytes 131104 | tf_op jit(solution)/shard_map/all_to_all | solution.py:28
  21.9 1.2 %shard_map.113 = f32[16,8,256]{2,1,0:T(8,128)S(1)} custom-call(s32[2,48]{1,0:T(2,128)S(1)} %pad_add_fusion.2.index_ref, bf16[32,8,256]{2,1,0:T(8,128)(2,1)S(1)} %all-to-all-done.source_ref, bf16[48,128,128]{2,1,0:T(8,128)(2,1)S(1)} %broadcast_select_fusion.tiles_ref), custom_call_target="tpu_custom_call" | custom-call | flops 12582912 | bytes 1572864 | tf_op jit(solution)/shard_map/pallas_call | solution.py:67
  23.2 3.7 %all-gather = f32[32,8,256]{2,1,0:T(8,128)S(1)} all-gather(f32[16,8,256]{2,1,0:T(8,128)S(1)} %shard_map.113), channel_id=2, replica_groups=mesh['z'=8,'core'=2,'col'=32] {'core'}, dimensions={0}, use_global_device_ids=true | all-gather | bytes 393216 | tf_op jit(solution)/shard_map/all_gather | solution.py:142
  26.9 24.4 %all_to_all.30 = f16[8,13,8,256]{3,2,1,0:T(8,128)(2,1)S(1)} all-to-all(f16[8,13,8,256]{3,2,1,0:T(8,128)(2,1)S(1)} %broadcast_in_dim.80), channel_id=1, replica_groups=mesh['z'=8,'core'=2,'col'=32] {'z'}, dimensions={0} | all-to-all | bytes 851968 | tf_op jit(solution)/shard_map/all_to_all | solution.py:28
  51.5 3.2 %all_gather.20.source_ref = bf16[16,8,256]{2,1,0:T(8,128)(2,1)S(1)} all-gather(bf16[8,8,256]{2,1,0:T(8,128)(2,1)S(1)} %get-tuple-element.18), channel_id=1, replica_groups=mesh['z'=8,'core'=2,'col'=32] {'core'}, dimensions={0}, use_global_device_ids=true | all-gather | bytes 98304 | tf_op jit(solution)/shard_map/all_gather | solution.py:158
  54.8 1.2 %shard_map.114 = f32[32,8,256]{2,1,0:T(8,128)S(1)} custom-call(s32[2,48]{1,0:T(2,128)S(1)} %pad_add_fusion.2.index_ref, bf16[16,8,256]{2,1,0:T(8,128)(2,1)S(1)} %all_gather.20.source_ref, bf16[48,128,128]{2,1,0:T(8,128)(2,1)S(1)} %broadcast_select_fusion.tiles_ref), custom_call_target="tpu_custom_call" | custom-call | flops 12582912 | bytes 1572864 | tf_op jit(solution)/shard_map/pallas_call | solution.py:67
  56.0 12.4 %all_to_all.31 = f16[32,8,256]{2,1,0:T(8,128)(2,1)S(1)} all-to-all(f16[32,8,256]{2,1,0:T(8,128)(2,1)S(1)} %convert_element_type.110), channel_id=1, replica_groups=mesh['z'=8,'core'=2,'col'=32] {'col'}, dimensions={0} | all-to-all | bytes 262144 | tf_op jit(solution)/shard_map/all_to_all | solution.py:162
  68.5 13.0 %all_to_all.32.source_ref = bf16[32,8,256]{2,1,0:T(8,128)(2,1)S(1)} all-to-all(bf16[32,8,256]{2,1,0:T(8,128)(2,1)S(1)} %broadcast_in_dim.81), channel_id=1, replica_groups=mesh['z'=8,'core'=2,'col'=32] {'col'}, dimensions={0} | all-to-all | bytes 262144 | tf_op jit(solution)/shard_map/all_to_all | solution.py:28
  81.5 1.2 %shard_map.115 = f32[16,8,256]{2,1,0:T(8,128)S(1)} custom-call(s32[2,48]{1,0:T(2,128)S(1)} %pad_add_fusion.2.index_ref, bf16[32,8,256]{2,1,0:T(8,128)(2,1)S(1)} %all_to_all.32.source_ref, bf16[48,128,128]{2,1,0:T(8,128)(2,1)S(1)} %broadcast_select_fusion.tiles_ref), custom_call_target="tpu_custom_call" | custom-call | flops 12582912 | bytes 1572864 | tf_op jit(solution)/shard_map/pallas_call | solution.py:67
  82.7 4.5 %all-gather.1 = f32[32,8,256]{2,1,0:T(8,128)S(1)} all-gather(f32[16,8,256]{2,1,0:T(8,128)S(1)} %shard_map.115), channel_id=3, replica_groups=mesh['z'=8,'core'=2,'col'=32] {'core'}, dimensions={0}, use_global_device_ids=true | all-gather | bytes 393216 | tf_op jit(solution)/shard_map/all_gather | solution.py:142
  87.3 14.8 %all_to_all.33 = f16[8,8,8,256]{3,2,1,0:T(8,128)(2,1)S(1)} all-to-all(f16[8,8,8,256]{3,2,1,0:T(8,128)(2,1)S(1)} %broadcast_in_dim.82), channel_id=1, replica_groups=mesh['z'=8,'core'=2,'col'=32] {'z'}, dimensions={0} | all-to-all | bytes 524288 | tf_op jit(solution)/shard_map/all_to_all | solution.py:28
  102.1 2.0 %all_gather.23.source_ref = bf16[16,8,256]{2,1,0:T(8,128)(2,1)S(1)} all-gather(bf16[8,8,256]{2,1,0:T(8,128)(2,1)S(1)} %get-tuple-element.16), channel_id=1, replica_groups=mesh['z'=8,'core'=2,'col'=32] {'core'}, dimensions={0}, use_global_device_ids=true | all-gather | bytes 98304 | tf_op jit(solution)/shard_map/all_gather | solution.py:158
  104.1 1.2 %shard_map.116 = f32[32,8,256]{2,1,0:T(8,128)S(1)} custom-call(s32[2,48]{1,0:T(2,128)S(1)} %pad_add_fusion.2.index_ref, bf16[16,8,256]{2,1,0:T(8,128)(2,1)S(1)} %all_gather.23.source_ref, bf16[48,128,128]{2,1,0:T(8,128)(2,1)S(1)} %broadcast_select_fusion.tiles_ref), custom_call_target="tpu_custom_call" | custom-call | flops 12582912 | bytes 1572864 | tf_op jit(solution)/shard_map/pallas_call | solution.py:67
  105.4 12.3 %all_to_all.34 = f16[32,8,256]{2,1,0:T(8,128)(2,1)S(1)} all-to-all(f16[32,8,256]{2,1,0:T(8,128)(2,1)S(1)} %convert_element_type.116), channel_id=1, replica_groups=mesh['z'=8,'core'=2,'col'=32] {'col'}, dimensions={0} | all-to-all | bytes 262144 | tf_op jit(solution)/shard_map/all_to_all | solution.py:162
  117.7 0.6 shard_map.117
  (34 shorter events, 0.5 us)
Async XLA Ops:
  2.1 19.9 %all-to-all-start = ((bf16[32,8,256]{2,1,0:T(8,128)(2,1)}), bf16[32,8,256]{2,1,0:T(8,128)(2,1)S(1)}, u32[]{:S(2)}, u32[]{:S(2)}) async-start(bf16[32,8,256]{2,1,0:T(8,128)(2,1)} %add_convert_fusion), calls=%async_computation | async-start | bytes 262144 | tf_op jit(solution)/shard_map/all_to_all | solution.py:28

commit v8 on v7

--- a/solution.py
+++ b/solution.py
@@ -29,11 +29,11 @@
 
 
 def pack(parts):
-    size = sum(part.shape[0] for part in parts)
-    total, at = 0, 0
+    rows, lanes = sum(part.shape[0] for part in parts), max(part.shape[1] for part in parts)
+    total, at = 0.0, 0
     for part in parts:
-        rest = [(0, 0)] * (part.ndim - 1)
-        total = total + jnp.pad(part, [(at, size - at - part.shape[0]), *rest])
+        padded = jnp.pad(part, ((at, rows - at - part.shape[0]), (0, lanes - part.shape[1])))
+        total = total + padded.astype(jnp.float32)
         at += part.shape[0]
     return lax.optimization_barrier(total)
 
@@ -114,11 +114,13 @@
     live = jnp.arange(slots, dtype=jnp.int32) < tile_count[0]
     tiles = jnp.where(live[:, None, None], tiles, jnp.zeros_like(tiles))
 
-    fields = pack([primal, cost, lax.optimization_barrier(dual), upper[None], rhs[None]])
-    x_own, cost_own, y, upper_own, rhs_own = jnp.split(fields, [width, 2 * width, 3 * width, 3 * width + 1])
-    kind, rows, cols = jnp.split(pack([row_kind, tile_rows, tile_cols]), [piece, piece + slots])
-    floor = jnp.where(kind == 1, 0.0, jnp.finfo(jnp.float32).min)
-    upper_own, rhs_own, floor = (jnp.broadcast_to(row, primal.shape) for row in (upper_own, rhs_own, floor[None]))
+    rows_of = [upper, rhs, row_kind, tile_rows, tile_cols]
+    fields = pack([primal, cost, lax.optimization_barrier(dual), *(vector[None] for vector in rows_of)])
+    ends = [width, 2 * width, *(3 * width + i for i in range(len(rows_of)))]
+    x_own, cost_own, y, upper_own, rhs_own, kind, rows, cols = jnp.split(fields, ends)
+    rows, cols = (row[0, :slots].astype(jnp.int32) for row in (rows, cols))
+    floor = jnp.where(kind == 1.0, 0.0, jnp.finfo(jnp.float32).min)
+    upper_own, rhs_own, floor = (jnp.broadcast_to(row, primal.shape) for row in (upper_own, rhs_own, floor))
     owner = cols // per_piece
     tile_at = ((owner % CORES) * planes + owner // CORES) * per_piece + cols % per_piece
     index = jnp.stack([rows, tile_at])

time: 119 us -> 119 us (level)
  transfers between devices with their start and end apart: 1 -> 1, of which waited for: 1 -> 1; matrix products, arithmetic and copies ran while one was open for 3% -> 2% of each run, Pallas kernels for 0% -> 0%
where the time goes in v8:
time: 119 us; the launch traced here: 118 us
  blocking collectives  90.4 us (76%)
  starting transfers between devices  10.5 us (9%)
  waiting for transfers between devices  6.01 us (5%)
  Pallas kernels  5.53 us (5%)
  other arithmetic  4.41 us (4%)
  between operations  1.47 us (1%)
    all_to_all x3, blocking collectives, to_all(): return lax.all_to_all(copies, axis, 0, 0, tiled=True)  52.2 us
    all_to_all x2, blocking collectives, body(): lax.all_to_all((partial_image * scale).astype(jnp.float16), 'col', 0, 0,...  24.7 us
    all_to_all x1, starting transfers between devices, to_all(): return lax.all_to_all(copies, axis, 0, 0, tiled=True)  10.5 us
    all_gather x2, blocking collectives, body(): lax.all_gather(partial_grad, 'core', axis=0)  8.19 us
    all_to_all x1, waiting for transfers between devices, to_all(): return lax.all_to_all(copies, axis, 0, 0, tiled=True)  6.01 us
    all_gather x2, blocking collectives, body(): x_cols = lax.all_gather(xbar, 'core', axis=0, tiled=True)  5.23 us
    pallas_call x4, Pallas kernels, tile_products(): pl.pallas_call(functools.partial(tiles_kernel, contract, origins, targets...  4.91 us
  transfers between devices with their start and end apart: 1, of which 1 were waited for; matrix products, arithmetic and copies ran while one was open for 2% of the time, Pallas kernels for 0%

profile of v8, /device:TPU:1, one launch (start us, length us, event | category | flops | bytes accessed | tf_op | source)
XLA Modules:
  0.0 118.3 jit_solution(11297388616884982323)
XLA Ops:
  0.6 1.4 %add_convert_fusion = bf16[32,8,256]{2,1,0:T(8,128)(2,1)} fusion(f32[32]{0:T(128)S(1)} %bitcast.107, f32[8,256]{1,0:T(8,128)} %param.11), kind=kLoop, calls=%fused_computation.5 | loop fusion | flops 131072 | bytes 139392 | tf_op jit(solution)/shard_map/convert_element_type | solution.py:27
  2.1 10.5 %all-to-all-start = ((bf16[32,8,256]{2,1,0:T(8,128)(2,1)}), bf16[32,8,256]{2,1,0:T(8,128)(2,1)S(1)}, u32[]{:S(2)}, u32[]{:S(2)}) async-start(bf16[32,8,256]{2,1,0:T(8,128)(2,1)} %add_convert_fusion), calls=%async_computation | async-start | bytes 262144 | tf_op jit(solution)/shard_map/all_to_all | solution.py:28
  12.6 0.8 convert_add_fusion.2
  14.2 1.6 %broadcast_select_fusion.tiles_ref = bf16[48,128,128]{2,1,0:T(8,128)(2,1)S(1)} fusion(bf16[48,128,128]{2,1,0:T(8,128)(2,1)} %param.16, pred[48]{0:T(512)(128)(4,1)S(1)} %iota_compare_fusion.1), kind=kLoop, calls=%fused_computation | loop fusion | flops 786432 | bytes 3145776 | tf_op jit(solution)/shard_map/jit(_where)/select_n | solution.py:115
  15.8 0.1 constant_dynamic-update-slice_fusion
  15.9 6.0 %all-to-all-done.source_ref = bf16[32,8,256]{2,1,0:T(8,128)(2,1)S(1)} async-done(((bf16[32,8,256]{2,1,0:T(8,128)(2,1)}), bf16[32,8,256]{2,1,0:T(8,128)(2,1)S(1)}, u32[]{:S(2)}, u32[]{:S(2)}) %all-to-all-start) | async-done | bytes 131104 | tf_op jit(solution)/shard_map/all_to_all | solution.py:28
  21.9 1.2 %shard_map.113 = f32[16,8,256]{2,1,0:T(8,128)S(1)} custom-call(s32[2,48]{1,0:T(2,128)S(1)} %pad_add_fusion.index_ref, bf16[32,8,256]{2,1,0:T(8,128)(2,1)S(1)} %all-to-all-done.source_ref, bf16[48,128,128]{2,1,0:T(8,128)(2,1)S(1)} %broadcast_select_fusion.tiles_ref), custom_call_target="tpu_custom_call" | custom-call | flops 12582912 | bytes 1572864 | tf_op jit(solution)/shard_map/pallas_call | solution.py:67
  23.2 3.7 %all-gather = f32[32,8,256]{2,1,0:T(8,128)S(1)} all-gather(f32[16,8,256]{2,1,0:T(8,128)S(1)} %shard_map.113), channel_id=2, replica_groups=mesh['z'=8,'core'=2,'col'=32] {'core'}, dimensions={0}, use_global_device_ids=true | all-gather | bytes 393216 | tf_op jit(solution)/shard_map/all_gather | solution.py:144
  26.9 24.4 %all_to_all.30 = f16[8,13,8,256]{3,2,1,0:T(8,128)(2,1)S(1)} all-to-all(f16[8,13,8,256]{3,2,1,0:T(8,128)(2,1)S(1)} %broadcast_in_dim.94), channel_id=1, replica_groups=mesh['z'=8,'core'=2,'col'=32] {'z'}, dimensions={0} | all-to-all | bytes 851968 | tf_op jit(solution)/shard_map/all_to_all | solution.py:28
  51.5 3.2 %all_gather.20.source_ref = bf16[16,8,256]{2,1,0:T(8,128)(2,1)S(1)} all-gather(bf16[8,8,256]{2,1,0:T(8,128)(2,1)S(1)} %get-tuple-element.18), channel_id=1, replica_groups=mesh['z'=8,'core'=2,'col'=32] {'core'}, dimensions={0}, use_global_device_ids=true | all-gather | bytes 98304 | tf_op jit(solution)/shard_map/all_gather | solution.py:160
  54.8 1.2 %shard_map.114 = f32[32,8,256]{2,1,0:T(8,128)S(1)} custom-call(s32[2,48]{1,0:T(2,128)S(1)} %pad_add_fusion.index_ref, bf16[16,8,256]{2,1,0:T(8,128)(2,1)S(1)} %all_gather.20.source_ref, bf16[48,128,128]{2,1,0:T(8,128)(2,1)S(1)} %broadcast_select_fusion.tiles_ref), custom_call_target="tpu_custom_call" | custom-call | flops 12582912 | bytes 1572864 | tf_op jit(solution)/shard_map/pallas_call | solution.py:67
  56.0 12.4 %all_to_all.31 = f16[32,8,256]{2,1,0:T(8,128)(2,1)S(1)} all-to-all(f16[32,8,256]{2,1,0:T(8,128)(2,1)S(1)} %convert_element_type.132), channel_id=1, replica_groups=mesh['z'=8,'core'=2,'col'=32] {'col'}, dimensions={0} | all-to-all | bytes 262144 | tf_op jit(solution)/shard_map/all_to_all | solution.py:164
  68.5 13.0 %all_to_all.32.source_ref = bf16[32,8,256]{2,1,0:T(8,128)(2,1)S(1)} all-to-all(bf16[32,8,256]{2,1,0:T(8,128)(2,1)S(1)} %broadcast_in_dim.95), channel_id=1, replica_groups=mesh['z'=8,'core'=2,'col'=32] {'col'}, dimensions={0} | all-to-all | bytes 262144 | tf_op jit(solution)/shard_map/all_to_all | solution.py:28
  81.5 1.2 %shard_map.115 = f32[16,8,256]{2,1,0:T(8,128)S(1)} custom-call(s32[2,48]{1,0:T(2,128)S(1)} %pad_add_fusion.index_ref, bf16[32,8,256]{2,1,0:T(8,128)(2,1)S(1)} %all_to_all.32.source_ref, bf16[48,128,128]{2,1,0:T(8,128)(2,1)S(1)} %broadcast_select_fusion.tiles_ref), custom_call_target="tpu_custom_call" | custom-call | flops 12582912 | bytes 1572864 | tf_op jit(solution)/shard_map/pallas_call | solution.py:67
  82.7 4.5 %all-gather.1 = f32[32,8,256]{2,1,0:T(8,128)S(1)} all-gather(f32[16,8,256]{2,1,0:T(8,128)S(1)} %shard_map.115), channel_id=3, replica_groups=mesh['z'=8,'core'=2,'col'=32] {'core'}, dimensions={0}, use_global_device_ids=true | all-gather | bytes 393216 | tf_op jit(solution)/shard_map/all_gather | solution.py:144
  87.3 14.8 %all_to_all.33 = f16[8,8,8,256]{3,2,1,0:T(8,128)(2,1)S(1)} all-to-all(f16[8,8,8,256]{3,2,1,0:T(8,128)(2,1)S(1)} %broadcast_in_dim.96), channel_id=1, replica_groups=mesh['z'=8,'core'=2,'col'=32] {'z'}, dimensions={0} | all-to-all | bytes 524288 | tf_op jit(solution)/shard_map/all_to_all | solution.py:28
  102.1 2.0 %all_gather.23.source_ref = bf16[16,8,256]{2,1,0:T(8,128)(2,1)S(1)} all-gather(bf16[8,8,256]{2,1,0:T(8,128)(2,1)S(1)} %get-tuple-element.16), channel_id=1, replica_groups=mesh['z'=8,'core'=2,'col'=32] {'core'}, dimensions={0}, use_global_device_ids=true | all-gather | bytes 98304 | tf_op jit(solution)/shard_map/all_gather | solution.py:160
  104.1 1.2 %shard_map.116 = f32[32,8,256]{2,1,0:T(8,128)S(1)} custom-call(s32[2,48]{1,0:T(2,128)S(1)} %pad_add_fusion.index_ref, bf16[16,8,256]{2,1,0:T(8,128)(2,1)S(1)} %all_gather.23.source_ref, bf16[48,128,128]{2,1,0:T(8,128)(2,1)S(1)} %broadcast_select_fusion.tiles_ref), custom_call_target="tpu_custom_call" | custom-call | flops 12582912 | bytes 1572864 | tf_op jit(solution)/shard_map/pallas_call | solution.py:67
  105.4 12.3 %all_to_all.34 = f16[32,8,256]{2,1,0:T(8,128)(2,1)S(1)} all-to-all(f16[32,8,256]{2,1,0:T(8,128)(2,1)S(1)} %convert_element_type.138), channel_id=1, replica_groups=mesh['z'=8,'core'=2,'col'=32] {'col'}, dimensions={0} | all-to-all | bytes 262144 | tf_op jit(solution)/shard_map/all_to_all | solution.py:164
  117.7 0.6 shard_map.117
  (35 shorter events, 0.6 us)
Async XLA Ops:
  2.1 19.9 %all-to-all-start = ((bf16[32,8,256]{2,1,0:T(8,128)(2,1)}), bf16[32,8,256]{2,1,0:T(8,128)(2,1)S(1)}, u32[]{:S(2)}, u32[]{:S(2)}) async-start(bf16[32,8,256]{2,1,0:T(8,128)(2,1)} %add_convert_fusion), calls=%async_computation | async-start | bytes 262144 | tf_op jit(solution)/shard_map/all_to_all | solution.py:28

commit v9 on v8

--- a/solution.py
+++ b/solution.py
@@ -22,9 +22,8 @@
     return 2.0 ** min(0, math.floor(math.log2(0.95 * HALF_MAX / bound)))
 
 
-def to_all(piece, axis, dtype, fresh=False):
-    zeros = lax.optimization_barrier(jnp.zeros((lax.axis_size(axis), 1, 1), piece.dtype)) if fresh else 0.0
-    copies = jnp.broadcast_to(piece[None] + zeros, (lax.axis_size(axis), *piece.shape)).astype(dtype)
+def to_all(piece, axis, dtype):
+    copies = jnp.broadcast_to(piece[None], (lax.axis_size(axis), *piece.shape)).astype(dtype)
     return lax.all_to_all(copies, axis, 0, 0, tiled=True)
 
 
@@ -50,11 +49,11 @@
         return lax.dot_general(piece, tile, (((1,), (contract,)), ((), ())), preferred_element_type=jnp.float32)
 
     out_ref[...] = jnp.zeros_like(out_ref)
-    together = 2 if contract == 1 and slots % 2 == 0 else 1
+    together = 2 if slots % 2 == 0 else 1
     for slot in range(0, slots, together):
         pieces = [source_ref[place(origins, slot + i)] for i in range(together)]
         tiles = [tiles_ref[slot + i] for i in range(together)]
-        found = product(jnp.concatenate(pieces, 0), jnp.concatenate(tiles, 0)) if together > 1 else product(pieces[0], tiles[0])
+        found = product(jnp.concatenate(pieces, 0), jnp.concatenate(tiles, 1 - contract)) if together > 1 else product(pieces[0], tiles[0])
         for i in range(together):
             products_ref[slot + i] = found[i * width : (i + 1) * width, i * LANES : (i + 1) * LANES]
     for slot in range(slots):
@@ -133,7 +132,7 @@
     y_max = DUAL_MAX
     x_half = None
     for step in range(ITERS):
-        y_rows = to_all(y_sends, "col", jnp.bfloat16, fresh=step == 0)
+        y_rows = to_all(y_sends, "col", jnp.bfloat16)
         if step == 0:
             y_rows, index, tiles, state, lifted, pull, floor = lax.optimization_barrier(
                 (y_rows, index, tiles, state, lifted, pull, floor)
@@ -141,8 +140,9 @@
             raised, images, steps = lifted, [], []
         partial_grad = tile_products(0, ROW_AT, COL_AT, index, y_rows, tiles, CORES * planes)
 
-        both = lax.all_gather(partial_grad, "core", axis=0).reshape(CORES, CORES, planes, width, piece)
-        mine = jnp.sum(lax.dynamic_index_in_dim(both, core, 1, keepdims=False), axis=0)
+        halves = partial_grad.reshape(CORES, planes, width, piece)
+        passed = lax.all_gather(lax.dynamic_index_in_dim(halves, 1 - core, 0, keepdims=False), "core", axis=0)
+        mine = sum(lax.dynamic_index_in_dim(part, at, 0, keepdims=False) for part, at in ((halves, core), (passed, 1 - core)))
         scale = step_down(CORES * min(slots, row_tiles) * LANES * TILE_MAX * y_max)
         sends = (mine * scale).astype(jnp.float16)
         if step == 0:

time: 119 us -> 119 us (level)
  no operation moved by 1% of the time
where the time goes in v9:
time: 119 us; the launch traced here: 118 us
  blocking collectives  90.2 us (76%)
  starting transfers between devices  10.5 us (9%)
  waiting for transfers between devices  6 us (5%)
  Pallas kernels  5.49 us (5%)
  other arithmetic  3.66 us (3%)
  between operations  1.49 us (1%)
    all_to_all x3, blocking collectives, to_all(): return lax.all_to_all(copies, axis, 0, 0, tiled=True)  52.3 us
    all_to_all x2, blocking collectives, body(): lax.all_to_all((partial_image * scale).astype(jnp.float16), 'col', 0, 0,...  24.7 us
    all_to_all x1, starting transfers between devices, to_all(): return lax.all_to_all(copies, axis, 0, 0, tiled=True)  10.5 us
    all_gather x2, blocking collectives, body(): lax.all_gather(lax.dynamic_index_in_dim(halves, 1 - core, 0, keepdims=Fal...  8.04 us
    all_to_all x1, waiting for transfers between devices, to_all(): return lax.all_to_all(copies, axis, 0, 0, tiled=True)  6 us
    all_gather x2, blocking collectives, body(): x_cols = lax.all_gather(xbar, 'core', axis=0, tiled=True)  5.19 us
    pallas_call x4, Pallas kernels, tile_products(): pl.pallas_call(functools.partial(tiles_kernel, contract, origins, targets...  4.87 us
  transfers between devices with their start and end apart: 1, of which 1 were waited for; matrix products, arithmetic and copies ran while one was open for 2% of the time, Pallas kernels for 0%

profile of v9, /device:TPU:1, one launch (start us, length us, event | category | flops | bytes accessed | tf_op | source)
XLA Modules:
  0.0 118.1 jit_solution(12739464634259212166)
XLA Ops:
  0.6 0.7 convert_element_type.112
  1.3 0.6 broadcast_in_dim.82
  2.0 10.5 %all-to-all-start = ((bf16[32,8,256]{2,1,0:T(8,128)(2,1)}), bf16[32,8,256]{2,1,0:T(8,128)(2,1)S(1)}, u32[]{:S(2)}, u32[]{:S(2)}) async-start(bf16[32,8,256]{2,1,0:T(8,128)(2,1)} %broadcast_in_dim.82), calls=%async_computation | async-start | bytes 262144 | tf_op jit(solution)/shard_map/all_to_all | solution.py:27
  12.5 0.8 convert_add_fusion.2
  14.1 1.6 %broadcast_select_fusion.tiles_ref = bf16[48,128,128]{2,1,0:T(8,128)(2,1)S(1)} fusion(bf16[48,128,128]{2,1,0:T(8,128)(2,1)} %param.16, pred[48]{0:T(512)(128)(4,1)S(1)} %iota_compare_fusion.1), kind=kLoop, calls=%fused_computation | loop fusion | flops 786432 | bytes 3145776 | tf_op jit(solution)/shard_map/jit(_where)/select_n | solution.py:114
  15.7 0.1 constant_dynamic-update-slice_fusion
  15.8 6.0 %all-to-all-done.source_ref = bf16[32,8,256]{2,1,0:T(8,128)(2,1)S(1)} async-done(((bf16[32,8,256]{2,1,0:T(8,128)(2,1)}), bf16[32,8,256]{2,1,0:T(8,128)(2,1)S(1)}, u32[]{:S(2)}, u32[]{:S(2)}) %all-to-all-start) | async-done | bytes 131104 | tf_op jit(solution)/shard_map/all_to_all | solution.py:27
  21.8 1.2 %shard_map.113 = f32[16,8,256]{2,1,0:T(8,128)S(1)} custom-call(s32[2,48]{1,0:T(2,128)S(1)} %pad_add_fusion.index_ref, bf16[32,8,256]{2,1,0:T(8,128)(2,1)S(1)} %all-to-all-done.source_ref, bf16[48,128,128]{2,1,0:T(8,128)(2,1)S(1)} %broadcast_select_fusion.tiles_ref), custom_call_target="tpu_custom_call" | custom-call | flops 12582912 | bytes 1572864 | tf_op jit(solution)/shard_map/pallas_call | solution.py:66
  23.1 3.6 %all_gather.14 = f32[2,8,8,256]{3,2,1,0:T(8,128)S(1)} all-gather(f32[1,8,8,256]{3,2,1,0:T(8,128)S(1)} %constant_dynamic-slice_fusion), channel_id=1, replica_groups=mesh['z'=8,'core'=2,'col'=32] {'core'}, dimensions={0}, use_global_device_ids=true | all-gather | bytes 196608 | tf_op jit(solution)/shard_map/all_gather | solution.py:144
  26.8 24.5 %all_to_all.30 = f16[8,13,8,256]{3,2,1,0:T(8,128)(2,1)S(1)} all-to-all(f16[8,13,8,256]{3,2,1,0:T(8,128)(2,1)S(1)} %broadcast_in_dim.98), channel_id=1, replica_groups=mesh['z'=8,'core'=2,'col'=32] {'z'}, dimensions={0} | all-to-all | bytes 851968 | tf_op jit(solution)/shard_map/all_to_all | solution.py:27
  51.4 3.2 %all_gather.15.source_ref = bf16[16,8,256]{2,1,0:T(8,128)(2,1)S(1)} all-gather(bf16[8,8,256]{2,1,0:T(8,128)(2,1)S(1)} %get-tuple-element.18), channel_id=1, replica_groups=mesh['z'=8,'core'=2,'col'=32] {'core'}, dimensions={0}, use_global_device_ids=true | all-gather | bytes 98304 | tf_op jit(solution)/shard_map/all_gather | solution.py:160
  54.6 1.2 %shard_map.114 = f32[32,8,256]{2,1,0:T(8,128)S(1)} custom-call(s32[2,48]{1,0:T(2,128)S(1)} %pad_add_fusion.index_ref, bf16[16,8,256]{2,1,0:T(8,128)(2,1)S(1)} %all_gather.15.source_ref, bf16[48,128,128]{2,1,0:T(8,128)(2,1)S(1)} %broadcast_select_fusion.tiles_ref), custom_call_target="tpu_custom_call" | custom-call | flops 12582912 | bytes 1572864 | tf_op jit(solution)/shard_map/pallas_call | solution.py:66
  55.8 12.4 %all_to_all.31 = f16[32,8,256]{2,1,0:T(8,128)(2,1)S(1)} all-to-all(f16[32,8,256]{2,1,0:T(8,128)(2,1)S(1)} %convert_element_type.134), channel_id=1, replica_groups=mesh['z'=8,'core'=2,'col'=32] {'col'}, dimensions={0} | all-to-all | bytes 262144 | tf_op jit(solution)/shard_map/all_to_all | solution.py:164
  68.3 13.0 %all_to_all.32.source_ref = bf16[32,8,256]{2,1,0:T(8,128)(2,1)S(1)} all-to-all(bf16[32,8,256]{2,1,0:T(8,128)(2,1)S(1)} %broadcast_in_dim.99), channel_id=1, replica_groups=mesh['z'=8,'core'=2,'col'=32] {'col'}, dimensions={0} | all-to-all | bytes 262144 | tf_op jit(solution)/shard_map/all_to_all | solution.py:27
  81.3 1.2 %shard_map.115 = f32[16,8,256]{2,1,0:T(8,128)S(1)} custom-call(s32[2,48]{1,0:T(2,128)S(1)} %pad_add_fusion.index_ref, bf16[32,8,256]{2,1,0:T(8,128)(2,1)S(1)} %all_to_all.32.source_ref, bf16[48,128,128]{2,1,0:T(8,128)(2,1)S(1)} %broadcast_select_fusion.tiles_ref), custom_call_target="tpu_custom_call" | custom-call | flops 12582912 | bytes 1572864 | tf_op jit(solution)/shard_map/pallas_call | solution.py:66
  82.6 4.4 %all_gather.16 = f32[2,8,8,256]{3,2,1,0:T(8,128)S(1)} all-gather(f32[1,8,8,256]{3,2,1,0:T(8,128)S(1)} %constant_dynamic-slice_fusion.1), channel_id=1, replica_groups=mesh['z'=8,'core'=2,'col'=32] {'core'}, dimensions={0}, use_global_device_ids=true | all-gather | bytes 196608 | tf_op jit(solution)/shard_map/all_gather | solution.py:144
  87.1 14.8 %all_to_all.33 = f16[8,8,8,256]{3,2,1,0:T(8,128)(2,1)S(1)} all-to-all(f16[8,8,8,256]{3,2,1,0:T(8,128)(2,1)S(1)} %broadcast_in_dim.101), channel_id=1, replica_groups=mesh['z'=8,'core'=2,'col'=32] {'z'}, dimensions={0} | all-to-all | bytes 524288 | tf_op jit(solution)/shard_map/all_to_all | solution.py:27
  101.9 2.0 %all_gather.17.source_ref = bf16[16,8,256]{2,1,0:T(8,128)(2,1)S(1)} all-gather(bf16[8,8,256]{2,1,0:T(8,128)(2,1)S(1)} %get-tuple-element.16), channel_id=1, replica_groups=mesh['z'=8,'core'=2,'col'=32] {'core'}, dimensions={0}, use_global_device_ids=true | all-gather | bytes 98304 | tf_op jit(solution)/shard_map/all_gather | solution.py:160
  103.9 1.2 %shard_map.116 = f32[32,8,256]{2,1,0:T(8,128)S(1)} custom-call(s32[2,48]{1,0:T(2,128)S(1)} %pad_add_fusion.index_ref, bf16[16,8,256]{2,1,0:T(8,128)(2,1)S(1)} %all_gather.17.source_ref, bf16[48,128,128]{2,1,0:T(8,128)(2,1)S(1)} %broadcast_select_fusion.tiles_ref), custom_call_target="tpu_custom_call" | custom-call | flops 12582912 | bytes 1572864 | tf_op jit(solution)/shard_map/pallas_call | solution.py:66
  105.1 12.3 %all_to_all.34 = f16[32,8,256]{2,1,0:T(8,128)(2,1)S(1)} all-to-all(f16[32,8,256]{2,1,0:T(8,128)(2,1)S(1)} %convert_element_type.140), channel_id=1, replica_groups=mesh['z'=8,'core'=2,'col'=32] {'col'}, dimensions={0} | all-to-all | bytes 262144 | tf_op jit(solution)/shard_map/all_to_all | solution.py:164
  117.5 0.6 shard_map.117
  (34 shorter events, 0.6 us)
Async XLA Ops:
  2.0 19.9 %all-to-all-start = ((bf16[32,8,256]{2,1,0:T(8,128)(2,1)}), bf16[32,8,256]{2,1,0:T(8,128)(2,1)S(1)}, u32[]{:S(2)}, u32[]{:S(2)}) async-start(bf16[32,8,256]{2,1,0:T(8,128)(2,1)} %broadcast_in_dim.82), calls=%async_computation | async-start | bytes 262144 | tf_op jit(solution)/shard_map/all_to_all | solution.py:27

commit v10 on v9

--- a/solution.py
+++ b/solution.py
@@ -140,9 +140,8 @@
             raised, images, steps = lifted, [], []
         partial_grad = tile_products(0, ROW_AT, COL_AT, index, y_rows, tiles, CORES * planes)
 
-        halves = partial_grad.reshape(CORES, planes, width, piece)
-        passed = lax.all_gather(lax.dynamic_index_in_dim(halves, 1 - core, 0, keepdims=False), "core", axis=0)
-        mine = sum(lax.dynamic_index_in_dim(part, at, 0, keepdims=False) for part, at in ((halves, core), (passed, 1 - core)))
+        both = lax.all_gather(partial_grad, "core", axis=0).reshape(CORES, CORES, planes, width, piece)
+        mine = jnp.sum(lax.dynamic_index_in_dim(both, core, 1, keepdims=False), axis=0)
         scale = step_down(CORES * min(slots, row_tiles) * LANES * TILE_MAX * y_max)
         sends = (mine * scale).astype(jnp.float16)
         if step == 0:

time: 119 us -> 119 us (level)
  no operation moved by 1% of the time
where the time goes in v10:
time: 119 us; the launch traced here: 118 us
  blocking collectives  90.4 us (76%)
  starting transfers between devices  10.5 us (9%)
  waiting for transfers between devices  6.01 us (5%)
  Pallas kernels  5.49 us (5%)
  other arithmetic  3.67 us (3%)
  between operations  1.47 us (1%)
    all_to_all x3, blocking collectives, to_all(): return lax.all_to_all(copies, axis, 0, 0, tiled=True)  52.2 us
    all_to_all x2, blocking collectives, body(): lax.all_to_all((partial_image * scale).astype(jnp.float16), 'col', 0, 0,...  24.7 us
    all_to_all x1, starting transfers between devices, to_all(): return lax.all_to_all(copies, axis, 0, 0, tiled=True)  10.5 us
    all_gather x2, blocking collectives, body(): lax.all_gather(partial_grad, 'core', axis=0)  8.21 us
    all_to_all x1, waiting for transfers between devices, to_all(): return lax.all_to_all(copies, axis, 0, 0, tiled=True)  6.01 us
    all_gather x2, blocking collectives, body(): x_cols = lax.all_gather(xbar, 'core', axis=0, tiled=True)  5.23 us
    pallas_call x4, Pallas kernels, tile_products(): pl.pallas_call(functools.partial(tiles_kernel, contract, origins, targets...  4.87 us
  transfers between devices with their start and end apart: 1, of which 1 were waited for; matrix products, arithmetic and copies ran while one was open for 2% of the time, Pallas kernels for 0%

profile of v10, /device:TPU:1, one launch (start us, length us, event | category | flops | bytes accessed | tf_op | source)
XLA Modules:
  0.0 118.2 jit_solution(14109246282156186241)
XLA Ops:
  0.6 0.7 convert_element_type.112
  1.3 0.6 broadcast_in_dim.80
  2.0 10.5 %all-to-all-start = ((bf16[32,8,256]{2,1,0:T(8,128)(2,1)}), bf16[32,8,256]{2,1,0:T(8,128)(2,1)S(1)}, u32[]{:S(2)}, u32[]{:S(2)}) async-start(bf16[32,8,256]{2,1,0:T(8,128)(2,1)} %broadcast_in_dim.80), calls=%async_computation | async-start | bytes 262144 | tf_op jit(solution)/shard_map/all_to_all | solution.py:27
  12.5 0.8 convert_add_fusion.2
  14.1 1.6 %broadcast_select_fusion.tiles_ref = bf16[48,128,128]{2,1,0:T(8,128)(2,1)S(1)} fusion(bf16[48,128,128]{2,1,0:T(8,128)(2,1)} %param.16, pred[48]{0:T(512)(128)(4,1)S(1)} %iota_compare_fusion.1), kind=kLoop, calls=%fused_computation | loop fusion | flops 786432 | bytes 3145776 | tf_op jit(solution)/shard_map/jit(_where)/select_n | solution.py:114
  15.7 0.1 constant_dynamic-update-slice_fusion
  15.8 6.0 %all-to-all-done.source_ref = bf16[32,8,256]{2,1,0:T(8,128)(2,1)S(1)} async-done(((bf16[32,8,256]{2,1,0:T(8,128)(2,1)}), bf16[32,8,256]{2,1,0:T(8,128)(2,1)S(1)}, u32[]{:S(2)}, u32[]{:S(2)}) %all-to-all-start) | async-done | bytes 131104 | tf_op jit(solution)/shard_map/all_to_all | solution.py:27
  21.8 1.2 %shard_map.113 = f32[16,8,256]{2,1,0:T(8,128)S(1)} custom-call(s32[2,48]{1,0:T(2,128)S(1)} %pad_add_fusion.index_ref, bf16[32,8,256]{2,1,0:T(8,128)(2,1)S(1)} %all-to-all-done.source_ref, bf16[48,128,128]{2,1,0:T(8,128)(2,1)S(1)} %broadcast_select_fusion.tiles_ref), custom_call_target="tpu_custom_call" | custom-call | flops 12582912 | bytes 1572864 | tf_op jit(solution)/shard_map/pallas_call | solution.py:66
  23.1 3.7 %all-gather = f32[32,8,256]{2,1,0:T(8,128)S(1)} all-gather(f32[16,8,256]{2,1,0:T(8,128)S(1)} %shard_map.113), channel_id=2, replica_groups=mesh['z'=8,'core'=2,'col'=32] {'core'}, dimensions={0}, use_global_device_ids=true | all-gather | bytes 393216 | tf_op jit(solution)/shard_map/all_gather | solution.py:143
  26.8 24.4 %all_to_all.30 = f16[8,13,8,256]{3,2,1,0:T(8,128)(2,1)S(1)} all-to-all(f16[8,13,8,256]{3,2,1,0:T(8,128)(2,1)S(1)} %broadcast_in_dim.96), channel_id=1, replica_groups=mesh['z'=8,'core'=2,'col'=32] {'z'}, dimensions={0} | all-to-all | bytes 851968 | tf_op jit(solution)/shard_map/all_to_all | solution.py:27
  51.4 3.2 %all_gather.20.source_ref = bf16[16,8,256]{2,1,0:T(8,128)(2,1)S(1)} all-gather(bf16[8,8,256]{2,1,0:T(8,128)(2,1)S(1)} %get-tuple-element.18), channel_id=1, replica_groups=mesh['z'=8,'core'=2,'col'=32] {'core'}, dimensions={0}, use_global_device_ids=true | all-gather | bytes 98304 | tf_op jit(solution)/shard_map/all_gather | solution.py:159
  54.6 1.2 %shard_map.114 = f32[32,8,256]{2,1,0:T(8,128)S(1)} custom-call(s32[2,48]{1,0:T(2,128)S(1)} %pad_add_fusion.index_ref, bf16[16,8,256]{2,1,0:T(8,128)(2,1)S(1)} %all_gather.20.source_ref, bf16[48,128,128]{2,1,0:T(8,128)(2,1)S(1)} %broadcast_select_fusion.tiles_ref), custom_call_target="tpu_custom_call" | custom-call | flops 12582912 | bytes 1572864 | tf_op jit(solution)/shard_map/pallas_call | solution.py:66
  55.9 12.4 %all_to_all.31 = f16[32,8,256]{2,1,0:T(8,128)(2,1)S(1)} all-to-all(f16[32,8,256]{2,1,0:T(8,128)(2,1)S(1)} %convert_element_type.133), channel_id=1, replica_groups=mesh['z'=8,'core'=2,'col'=32] {'col'}, dimensions={0} | all-to-all | bytes 262144 | tf_op jit(solution)/shard_map/all_to_all | solution.py:163
  68.4 13.0 %all_to_all.32.source_ref = bf16[32,8,256]{2,1,0:T(8,128)(2,1)S(1)} all-to-all(bf16[32,8,256]{2,1,0:T(8,128)(2,1)S(1)} %broadcast_in_dim.97), channel_id=1, replica_groups=mesh['z'=8,'core'=2,'col'=32] {'col'}, dimensions={0} | all-to-all | bytes 262144 | tf_op jit(solution)/shard_map/all_to_all | solution.py:27
  81.4 1.2 %shard_map.115 = f32[16,8,256]{2,1,0:T(8,128)S(1)} custom-call(s32[2,48]{1,0:T(2,128)S(1)} %pad_add_fusion.index_ref, bf16[32,8,256]{2,1,0:T(8,128)(2,1)S(1)} %all_to_all.32.source_ref, bf16[48,128,128]{2,1,0:T(8,128)(2,1)S(1)} %broadcast_select_fusion.tiles_ref), custom_call_target="tpu_custom_call" | custom-call | flops 12582912 | bytes 1572864 | tf_op jit(solution)/shard_map/pallas_call | solution.py:66
  82.6 4.5 %all-gather.1 = f32[32,8,256]{2,1,0:T(8,128)S(1)} all-gather(f32[16,8,256]{2,1,0:T(8,128)S(1)} %shard_map.115), channel_id=3, replica_groups=mesh['z'=8,'core'=2,'col'=32] {'core'}, dimensions={0}, use_global_device_ids=true | all-gather | bytes 393216 | tf_op jit(solution)/shard_map/all_gather | solution.py:143
  87.2 14.8 %all_to_all.33 = f16[8,8,8,256]{3,2,1,0:T(8,128)(2,1)S(1)} all-to-all(f16[8,8,8,256]{3,2,1,0:T(8,128)(2,1)S(1)} %broadcast_in_dim.98), channel_id=1, replica_groups=mesh['z'=8,'core'=2,'col'=32] {'z'}, dimensions={0} | all-to-all | bytes 524288 | tf_op jit(solution)/shard_map/all_to_all | solution.py:27
  102.0 2.0 %all_gather.23.source_ref = bf16[16,8,256]{2,1,0:T(8,128)(2,1)S(1)} all-gather(bf16[8,8,256]{2,1,0:T(8,128)(2,1)S(1)} %get-tuple-element.16), channel_id=1, replica_groups=mesh['z'=8,'core'=2,'col'=32] {'core'}, dimensions={0}, use_global_device_ids=true | all-gather | bytes 98304 | tf_op jit(solution)/shard_map/all_gather | solution.py:159
  104.0 1.2 %shard_map.116 = f32[32,8,256]{2,1,0:T(8,128)S(1)} custom-call(s32[2,48]{1,0:T(2,128)S(1)} %pad_add_fusion.index_ref, bf16[16,8,256]{2,1,0:T(8,128)(2,1)S(1)} %all_gather.23.source_ref, bf16[48,128,128]{2,1,0:T(8,128)(2,1)S(1)} %broadcast_select_fusion.tiles_ref), custom_call_target="tpu_custom_call" | custom-call | flops 12582912 | bytes 1572864 | tf_op jit(solution)/shard_map/pallas_call | solution.py:66
  105.3 12.3 %all_to_all.34 = f16[32,8,256]{2,1,0:T(8,128)(2,1)S(1)} all-to-all(f16[32,8,256]{2,1,0:T(8,128)(2,1)S(1)} %convert_element_type.139), channel_id=1, replica_groups=mesh['z'=8,'core'=2,'col'=32] {'col'}, dimensions={0} | all-to-all | bytes 262144 | tf_op jit(solution)/shard_map/all_to_all | solution.py:163
  117.6 0.6 shard_map.117
  (34 shorter events, 0.6 us)
Async XLA Ops:
  2.0 19.9 %all-to-all-start = ((bf16[32,8,256]{2,1,0:T(8,128)(2,1)}), bf16[32,8,256]{2,1,0:T(8,128)(2,1)S(1)}, u32[]{:S(2)}, u32[]{:S(2)}) async-start(bf16[32,8,256]{2,1,0:T(8,128)(2,1)} %broadcast_in_dim.80), calls=%async_computation | async-start | bytes 262144 | tf_op jit(solution)/shard_map/all_to_all | solution.py:27
